TPU v7x, 512 devices: a whole 4x8x8 slice. The times are simulated.
512 devices in a mesh: ctx: 128 (over y_hi, z, x, core), tp: 4 (over y_lo).
Axes of the slice: x: 4, y: 8 (y_hi: 2, y_lo: 4; y = y_hi * 4 + y_lo), z: 8, core: 2. Of those that a mesh axis runs over, the one named last changes fastest.
Arguments:
- streams: bfloat16 [3, 4096, 16384], P(None, 'tp', 'ctx'), may hold values from -6 to 6
- conv_weight: float32 [3, 7, 4096], P(None, None, 'tp'), may hold values from -2 to 2
- rates: float32 [512, 16], P('tp'), may hold values from 1.2207031e-05 to 0.05
- residues: float32 [512, 16], P('tp'), may hold values from -4 to 4
- skip: float32 [4096], P('tp'), may hold values from -4 to 4
- out_weight: bfloat16 [4096, 4096], P('ctx', 'tp'), may hold values from -0.09375 to 0.09375
Outputs:
- result: bfloat16 [16384, 4096], P('ctx', 'tp')
All inputs are finite; a program needn't handle non-finite values.
Results may differ from a plain program's by a relative error of at most 0.014.
Values may be sent and summed in bfloat16 or wider, within the bound.
A program may use at most 128 MiB of HBM per device.

v0:
```python
import math

import jax
import jax.numpy as jnp
from jax import lax
from jax.sharding import PartitionSpec as P


def from_behind(value, axis, steps):
    count = lax.axis_size(axis)
    leading, last = (max(0, -steps), min(count, count - steps))
    return lax.ppermute(value, axis, [(source, source + steps) for source in range(leading, last)])


def block_parts(signal, coefficient, rates):
    groups = coefficient.shape[0]
    channels, length = signal.shape
    group_width = channels // groups
    block_len = 128
    block_count = length // block_len
    blocks = signal.reshape(groups, group_width, block_count, block_len)
    position = jnp.arange(block_len, dtype=jnp.float32)
    centre = (block_len - 1.0) * 0.5
    left_factor = coefficient[:, :, None] * jnp.exp(-rates[:, :, None] * (position - centre))
    right_factor = jnp.exp(rates[:, :, None] * (position - centre))
    causal = (position[:, None] >= position[None, :]).astype(jnp.float32)
    toeplitz = (
        jnp.einsum("gni,gnj->gij", left_factor, right_factor, precision=lax.Precision.HIGHEST)
        * causal
    )
    inside = jnp.einsum("gij,gcbj->gcbi", toeplitz, blocks, precision=lax.Precision.HIGHEST)
    tail_decay = jnp.exp(-rates[:, :, None] * (block_len - 1.0 - position))
    block_ends = jnp.einsum("gnj,gcbj->gcbn", tail_decay, blocks, precision=lax.Precision.HIGHEST)
    block_index = jnp.arange(block_count, dtype=jnp.float32)
    lag = block_index[:, None] - block_index[None, :]
    earlier_mask = (lag >= 1.0).astype(jnp.float32)
    steps_back = jnp.maximum(lag - 1.0, 0.0)
    carry_matrix = jnp.exp(-rates[:, :, None, None] * block_len * steps_back) * earlier_mask
    entering = jnp.einsum(
        "gnab,gcbn->gcan", carry_matrix, block_ends, precision=lax.Precision.HIGHEST
    )
    last_decay = jnp.exp(-rates[:, :, None] * block_len * (block_count - 1.0 - block_index))
    segment_end = jnp.einsum(
        "gnb,gcbn->gcn", last_decay, block_ends, precision=lax.Precision.HIGHEST
    )
    return (inside, entering, segment_end)


def finish_conv(inside, entering, coefficient, rates):
    groups, group_width, block_count, block_len = inside.shape
    position = jnp.arange(block_len, dtype=jnp.float32)
    lift_out = coefficient[:, :, None] * jnp.exp(-rates[:, :, None] * (position + 1.0))
    total = inside + jnp.einsum(
        "gni,gcbn->gcbi", lift_out, entering, precision=lax.Precision.HIGHEST
    )
    return total.reshape(groups * group_width, block_count * block_len)


def local(streams, conv_weight, rates, residues, skip, out_weight):
    tap_count = conv_weight.shape[1]
    rim_width = tap_count - 1
    length = streams.shape[2]
    tail_rows = jnp.swapaxes(streams[:, :, length - rim_width :], 1, 2)
    before = from_behind(tail_rows, "ctx", 1)
    extended = jnp.concatenate([jnp.swapaxes(before, 1, 2), streams], axis=2)
    filtered = conv_weight[:, 0, :, None] * extended[:, :, rim_width:].astype(jnp.float32)
    for shift_by in range(1, tap_count):
        filtered = filtered + conv_weight[:, shift_by, :, None] * extended[
            :, :, rim_width - shift_by : rim_width - shift_by + length
        ].astype(jnp.float32)
    queries = filtered[0]
    gated_in = (filtered[1] * filtered[2]).astype(jnp.bfloat16)
    gated_wide = gated_in.astype(jnp.float32)
    coefficient = residues * jnp.sqrt(2.0 * rates) / math.sqrt(rates.shape[1])
    by_channel = lax.all_to_all(gated_in, "ctx", split_axis=0, concat_axis=1, tiled=True)
    per_device = rates.shape[0] // lax.axis_size("ctx")
    first_group = lax.axis_index("ctx") * per_device
    coef_mine = lax.dynamic_slice_in_dim(coefficient, first_group, per_device, 0)
    rates_mine = lax.dynamic_slice_in_dim(rates, first_group, per_device, 0)
    inside, entering, segment_end = block_parts(
        by_channel.astype(jnp.float32), coef_mine, rates_mine
    )
    filtered_all = finish_conv(inside, entering, coef_mine, rates_mine)
    conv_out = lax.all_to_all(filtered_all, "ctx", split_axis=1, concat_axis=0, tiled=True)
    mixed_out = (queries * (conv_out + skip[:, None] * gated_wide)).astype(jnp.bfloat16)
    features = lax.all_gather(mixed_out, "tp", axis=0, tiled=True)
    summed = lax.dot_general(
        features,
        lax.all_gather(out_weight, "ctx", axis=0, tiled=True),
        (((0,), (0,)), ((), ())),
        preferred_element_type=jnp.float32,
    )
    return summed.astype(jnp.bfloat16)


def solution(mesh):
    return jax.shard_map(
        local,
        mesh=mesh,
        in_specs=(
            P(None, "tp", "ctx"),
            P(None, None, "tp"),
            P("tp", None),
            P("tp", None),
            P("tp"),
            P("ctx", "tp"),
        ),
        out_specs=P("ctx", "tp"),
        check_vma=False,
    )
```

profile of v0, /device:TPU:1, one launch (start us, length us, event | category | flops | bytes accessed | tf_op | source)
XLA Modules:
  0.0 293.7 jit_solution(14990521191751933927)
XLA Ops:
  6.5 1.5 slice.53
  8.0 0.3 copy.24
  8.3 4.5 %collective-permute-start = (bf16[3,6,1024]{2,1,0:T(8,128)(2,1)S(1)}, bf16[3,6,1024]{2,1,0:T(8,128)(2,1)S(1)}, u32[]{:S(2)}, u32[]{:S(2)}) collective-permute-start(bf16[3,6,1024]{2,1,0:T(8,128)(2,1)S(1)} %bitcast.64), channel_id=1, source_target_pairs={{0,4},{4,8},{8,12},{12,16},{16,20},{20,24},{24,28},{28,32},{32,36}... | collective-permute-start | bytes 110600 | tf_op jit(solution)/shard_map/ppermute | solution.py:12
  12.9 0.1 fusion.51
  13.1 0.2 fusion.27
  13.3 3.9 %collective-permute-done = bf16[3,6,1024]{2,1,0:T(8,128)(2,1)S(1)} collective-permute-done((bf16[3,6,1024]{2,1,0:T(8,128)(2,1)S(1)}, bf16[3,6,1024]{2,1,0:T(8,128)(2,1)S(1)}, u32[]{:S(2)}, u32[]{:S(2)}) %collective-permute-start) | collective-permute-done | bytes 36896 | tf_op jit(solution)/shard_map/ppermute | solution.py:12
  17.2 0.4 copy.12
  17.6 5.6 %multiply_add_fusion = f32[3,1024,128]{2,1,0:T(8,128)S(1)} fusion(bf16[3,1024,128]{2,1,0:T(8,128)(2,1)S(1)} %copy-done, bf16[3,1024,6]{2,1,0:T(8,128)(2,1)S(1)} %bitcast.62, f32[3,1024]{1,0:T(4,128)S(1)} %get-tuple-element.16, f32[3,1024]{1,0:T(4,128)S(1)} %get-tuple-element.17, f32[3,1024]{1,0:T(4,128)S(1)} %get-tuple-element.18, ...), kind=kLoop, calls=%fused_computation.10 | loop fusion | flops 14942208 | bytes 2482176 | tf_op jit(solution)/shard_map/add | solution.py:68
  23.2 0.8 fusion.55
  24.0 18.2 %all-to-all-start = ((bf16[128,8,128]{2,1,0:T(8,128)(2,1)}), bf16[128,8,128]{2,1,0:T(8,128)(2,1)S(1)}, u32[]{:S(2)}, u32[]{:S(2)}) async-start(bf16[128,8,128]{2,1,0:T(8,128)(2,1)} %fusion.55), calls=%async_computation | async-start | bytes 524288 | tf_op jit(solution)/shard_map/all_to_all | solution.py:75
  42.3 0.4 fusion
  42.7 17.0 %all-to-all-done = bf16[128,8,128]{2,1,0:T(8,128)(2,1)S(1)} async-done(((bf16[128,8,128]{2,1,0:T(8,128)(2,1)}), bf16[128,8,128]{2,1,0:T(8,128)(2,1)S(1)}, u32[]{:S(2)}, u32[]{:S(2)}) %all-to-all-start) | async-done | bytes 262176 | tf_op jit(solution)/shard_map/all_to_all | solution.py:75
  59.7 0.3 fusion.16
  60.0 1.9 convolution_bitcast_fusion
  61.9 0.4 fusion.18
  62.3 1.0 convolution_add_fusion
  63.3 0.3 copy.16
  63.6 29.5 %all_to_all.29 = f32[8,128,128]{2,0,1:T(8,128)S(1)} all-to-all(f32[8,128,128]{2,0,1:T(8,128)S(1)} %copy.16), channel_id=1, replica_groups=mesh['ctx'=128,'tp'=4] {'ctx'}, dimensions={1} | all-to-all | bytes 1048576 | tf_op jit(solution)/shard_map/all_to_all | solution.py:84
  93.1 0.9 fusion.11
  94.0 0.0 all-gather.5.cloned.1.call-start
  94.1 0.7 all-gather.5.cloned.1.call-update
  94.8 26.1 %all-gather.3.cloned.1.call-done = bf16[4096,128]{1,0:T(8,128)(2,1)} async-done(((bf16[1024,128]{1,0:T(8,128)(2,1)}), bf16[4096,128]{1,0:T(8,128)(2,1)}) %all-gather.3.cloned.1.call-update) | async-done | bytes 1048592 | tf_op jit(solution)/shard_map/all_gather | solution.py:86
  120.9 160.3 %all-gather.5.cloned.1.call-done = bf16[4096,1024]{1,0:T(8,128)(2,1)} async-done(((bf16[32,1024]{1,0:T(8,128)(2,1)}), bf16[4096,1024]{1,0:T(8,128)(2,1)}) %all-gather.5.cloned.1.call-update) | async-done | bytes 8388624 | tf_op jit(solution)/shard_map/all_gather | solution.py:89
  281.2 5.7 %convolution_convert_fusion = bf16[128,1024]{1,0:T(8,128)(2,1)} fusion(bf16[4096,128]{1,0:T(8,128)(2,1)} %all-gather.3.cloned.1.call-done, bf16[4096,1024]{1,0:T(8,128)(2,1)} %all-gather.5.cloned.1.call-done), kind=kOutput, calls=%fused_computation.12 | convolution fusion | flops 1073872896 | bytes 9699328 | tf_op jit(solution)/shard_map/dot_general | solution.py:87
  (22 shorter events, 0.2 us)
Async XLA Ops:
  6.5 6.4 %copy-start.1 = (f32[3,7,1024]{2,1,0:T(8,128)S(1)}, f32[3,7,1024]{2,1,0:T(8,128)}, u32[]{:S(2)}) copy-start(f32[3,7,1024]{2,1,0:T(8,128)} %param.7) | copy-start | bytes 258052
  6.5 6.5 %copy-start.3 = (f32[128,16]{0,1:T(8,128)S(1)}, f32[128,16]{0,1:T(8,128)}, u32[]{:S(2)}) copy-start(f32[128,16]{0,1:T(8,128)} %param.8) | copy-start | bytes 24580
  6.5 6.5 %copy-start.2 = (f32[128,16]{0,1:T(8,128)S(1)}, f32[128,16]{0,1:T(8,128)}, u32[]{:S(2)}) copy-start(f32[128,16]{0,1:T(8,128)} %param.9) | copy-start | bytes 24580
  6.5 11.1 %copy-start = (bf16[3,1024,128]{2,1,0:T(8,128)(2,1)S(1)}, bf16[3,1024,128]{2,1,0:T(8,128)(2,1)}, u32[]{:S(2)}) copy-start(bf16[3,1024,128]{2,1,0:T(8,128)(2,1)} %param.6) | copy-start | bytes 2359300
  8.3 8.9 %collective-permute-start = (bf16[3,6,1024]{2,1,0:T(8,128)(2,1)S(1)}, bf16[3,6,1024]{2,1,0:T(8,128)(2,1)S(1)}, u32[]{:S(2)}, u32[]{:S(2)}) collective-permute-start(bf16[3,6,1024]{2,1,0:T(8,128)(2,1)S(1)} %bitcast.64), channel_id=1, source_target_pairs={{0,4},{4,8},{8,12},{12,16},{16,20},{20,24},{24,28},{28,32},{32,36}... | collective-permute-start | bytes 110600 | tf_op jit(solution)/shard_map/ppermute | solution.py:12
  24.0 35.7 %all-to-all-start = ((bf16[128,8,128]{2,1,0:T(8,128)(2,1)}), bf16[128,8,128]{2,1,0:T(8,128)(2,1)S(1)}, u32[]{:S(2)}, u32[]{:S(2)}) async-start(bf16[128,8,128]{2,1,0:T(8,128)(2,1)} %fusion.55), calls=%async_computation | async-start | bytes 524288 | tf_op jit(solution)/shard_map/all_to_all | solution.py:75
  42.2 78.7 %all-gather.3.cloned.1.call-start = ((), (), s32[]{:S(2)}) async-start(), calls=%async_computation.2 | async-start | bytes 1310720 | tf_op jit(solution)/shard_map/all_gather | solution.py:86
  62.3 30.8 %copy-start.4 = (f32[1024]{0:T(1024)S(1)}, f32[1024]{0:T(1024)}, u32[]{:S(2)}) copy-start(f32[1024]{0:T(1024)} %param.10) | copy-start | bytes 12292
  94.0 187.2 %all-gather.5.cloned.1.call-start = ((), (), s32[]{:S(2)}) async-start(), calls=%async_computation.3 | async-start | bytes 8454144 | tf_op jit(solution)/shard_map/all_gather | solution.py:89
Sparse Core Ops, SparseCore 0:
  94.1 26.7 all-gather.2
  125.5 155.6 all-gather.4
where the time goes:
time: 294 us
  waiting for transfers between devices  208 us (71%)
  blocking collectives  29.5 us (10%)
  starting transfers between devices  22.8 us (8%)
  between operations  13.6 us (5%)
  matrix products  9.69 us (3%)
  other arithmetic  7.52 us (3%)
    all_gather x1, waiting for transfers between devices, local(): lax.all_gather(out_weight, 'ctx', axis=0, tiled=True)  160 us
    all_to_all x1, blocking collectives, local(): lax.all_to_all(filtered_all, 'ctx', split_axis=1, concat_axis=0, tiled=True)  29.5 us
    all_gather x1, waiting for transfers between devices, local(): features = lax.all_gather(mixed_out, 'tp', axis=0, tiled=True)  26.1 us
    all_to_all x1, starting transfers between devices, local(): lax.all_to_all(gated_in, 'ctx', split_axis=0, concat_axis=1, tiled=True)  18.2 us
    all_to_all x1, waiting for transfers between devices, local(): lax.all_to_all(gated_in, 'ctx', split_axis=0, concat_axis=1, tiled=True)  17 us
  transfers between devices with their start and end apart: 4, of which 4 were waited for; matrix products, arithmetic and copies ran while one was open for 0% of the time, Pallas kernels for 0%

commit v1 on v0

v1 whole, which is shorter than its diff:
```python
import functools
import math

import jax
import jax.numpy as jnp
from jax import lax
from jax.experimental import pallas as pl
from jax.experimental.pallas import tpu as pltpu
from jax.sharding import PartitionSpec as P

NZ, NX = 8, 4
LINE = NX * 2
LANES = 128
RIM = 8
HIGHEST = lax.Precision.HIGHEST


class Message:
    def __init__(self, sems, number, src, dst, land, to):
        send, recv = sems
        make = functools.partial(
            pltpu.make_async_remote_copy,
            send_sem=send.at[number],
            recv_sem=recv.at[number],
            device_id=to,
            device_id_type=pl.DeviceIdType.MESH,
        )
        self.out = make(src_ref=src, dst_ref=dst)
        self.into = make(src_ref=src, dst_ref=land)

    def start(self):
        self.out.start()

    def recv(self):
        self.into.wait_recv()

    def sent(self):
        self.out.wait_send()


def kernel(
    tap_count,
    streams,
    taps,
    rates,
    residues,
    skip,
    w_in,
    out,
    w,
    ext,
    rim,
    query,
    gated,
    conv,
    decay,
    coef,
    rate_chunks,
    ends,
    line_in,
    row_total,
    row_in,
    enter_out,
    enter_in,
    mixed,
    total,
    send_sems,
    recv_sems,
):
    poles = rates.shape[1]
    channels, tokens = streams.shape[1:]
    half = channels // 2
    rows = w_in.shape[0]
    ctx, tp = lax.axis_index("ctx"), lax.axis_index("tp")
    ctx_n, tp_n = lax.axis_size("ctx"), lax.axis_size("tp")
    core = ctx % 2
    x = (ctx // 2) % NX
    z = (ctx // LINE) % NZ
    y = ctx // (LINE * NZ)
    place = ctx % LINE
    row = ctx // LINE

    def at(y_=None, z_=None, x_=None, core_=None):
        y_ = y if y_ is None else y_
        z_ = z if z_ is None else z_
        x_ = x if x_ is None else x_
        core_ = core if core_ is None else core_
        return (((y_ * NZ + z_) * NX + x_) * 2 + core_, tp)

    def flip(value, bits):
        result = value * 0
        for bit in (1, 2, 4):
            digit = (value // bit) % 2
            result = result + bit * ((1 - digit) if bits & bit else digit)
        return result

    sems = (send_sems, recv_sems)
    count = [0]
    sent = []

    def message(src, dst, land, to):
        made = Message(sems, count[0], src, dst, land, to)
        count[0] += 1
        return made

    def start(made):
        made.start()
        sent.append(made)

    line_peers = [ctx - place + flip(place, m) for m in range(1, LINE)]
    row_peers = [
        ((y + dy) % 2 * NZ + flip(z, m)) * LINE + place
        for dy in range(2)
        for m in range(NZ)
        if (dy, m) != (0, 0)
    ]
    next_ctx, last_ctx = (ctx + 1) % ctx_n, (ctx + ctx_n - 1) % ctx_n
    peers = [(c, tp) for c in line_peers + row_peers + [next_ctx, last_ctx]]
    peers += [(ctx, (tp + 1) % tp_n), (ctx, (tp + tp_n - 1) % tp_n)]
    barrier = pltpu.get_barrier_semaphore()
    for peer in peers:
        pl.semaphore_signal(barrier, inc=1, device_id=peer, device_id_type=pl.DeviceIdType.MESH)
    pl.semaphore_wait(barrier, len(peers))

    groups = [(0, 1), (1, 2), (3, 2), (5, 2), (7, 1)]
    ups, downs = at(z_=(z + 1) % NZ), at(z_=(z + NZ - 1) % NZ)
    rights, lefts = at(x_=(x + 1) % NX), at(x_=(x + NX - 1) % NX)
    x_left, x_right = (x + NX - 1) % NX, (x + 1) % NX
    x_far = (x + 2) % NX
    sibling = at(core_=1 - core)
    top, bottom = pl.ds(0, rows // 2), pl.ds(rows // 2, rows // 2)

    across = message(
        w_in, w.at[y, 0, x, core], w.at[1 - y, 0, x, core], at(y_=1 - y)
    )
    start(across)
    w[y, 0, x, core] = w_in[...]

    def za(step):
        up_src, down_src = max(2 * step - 2, 0), max(2 * step - 3, 0)
        if step < 4:
            return (
                message(w.at[0, up_src, x, core], w.at[0, 2 * step, x, core], w.at[0, 2 * step, x, core], ups),
                message(w.at[0, down_src, x, core], w.at[0, 2 * step - 1, x, core], w.at[0, 2 * step - 1, x, core], downs),
            )
        return (
            message(w.at[0, 6, x, core, top], w.at[0, 7, x, core, top], w.at[0, 7, x, core, top], ups),
            message(w.at[0, 5, x, core, bottom], w.at[0, 7, x, core, bottom], w.at[0, 7, x, core, bottom], downs),
        )

    def xa(group):
        slots = pl.ds(*groups[group])
        mine = w.at[0, slots, x, core]
        return (
            message(mine, mine, w.at[0, slots, x_left, core], rights),
            message(mine, mine, w.at[0, slots, x_right, core], lefts),
        )

    def xa_far(group):
        slots = pl.ds(*groups[group])
        from_left = w.at[0, slots, x_left, core, top]
        from_right = w.at[0, slots, x_right, core, bottom]
        return (
            message(from_left, from_left, w.at[0, slots, x_far, core, top], rights),
            message(from_right, from_right, w.at[0, slots, x_far, core, bottom], lefts),
        )

    def xb():
        mine = w.at[1, 0, x, core]
        return (
            message(mine, mine, w.at[1, 0, x_left, core], rights),
            message(mine, mine, w.at[1, 0, x_right, core], lefts),
        )

    def xb_far():
        from_left = w.at[1, 0, x_left, core, top]
        from_right = w.at[1, 0, x_right, core, bottom]
        return (
            message(from_left, from_left, w.at[1, 0, x_far, core, top], rights),
            message(from_right, from_right, w.at[1, 0, x_far, core, bottom], lefts),
        )

    def zb(step):
        up_src, down_src = max(2 * step - 2, 0), max(2 * step - 3, 0)
        all_x = pl.ds(0, NX)
        if step < 4:
            return (
                message(w.at[1, up_src, all_x, core], w.at[1, 2 * step, all_x, core], w.at[1, 2 * step, all_x, core], ups),
                message(w.at[1, down_src, all_x, core], w.at[1, 2 * step - 1, all_x, core], w.at[1, 2 * step - 1, all_x, core], downs),
            )
        first, second = pl.ds(0, NX // 2), pl.ds(NX // 2, NX // 2)
        return (
            message(w.at[1, 6, first, core], w.at[1, 7, first, core], w.at[1, 7, first, core], ups),
            message(w.at[1, 5, second, core], w.at[1, 7, second, core], w.at[1, 7, second, core], downs),
        )

    def share(y_, group):
        slots = pl.ds(*groups[group])
        mine = w.at[y_, slots, pl.ds(0, NX), core]
        return (message(mine, mine, w.at[y_, slots, pl.ds(0, NX), 1 - core], sibling),)

    za_m = {s: za(s) for s in (1, 2, 3, 4)}
    xa_m = {g: xa(g) for g in range(5)}
    xaf_m = {g: xa_far(g) for g in range(5)}
    xb_m, xbf_m = xb(), xb_far()
    zb_m = {s: zb(s) for s in (1, 2, 3, 4)}
    share_m = {(y_, g): share(y_, g) for y_ in range(2) for g in range(5)}

    def start_all(pair):
        for made in pair:
            start(made)

    def recv_all(pair):
        for made in pair:
            made.recv()

    eye = (
        lax.broadcasted_iota(jnp.int32, (tokens, tokens), 0)
        == lax.broadcasted_iota(jnp.int32, (tokens, tokens), 1)
    ).astype(jnp.bfloat16)
    for s in range(3):
        ext[s, pl.ds(RIM, tokens), :] = lax.dot_general(
            eye, streams[s], (((1,), (1,)), ((), ())), preferred_element_type=jnp.float32
        )
    rim_m = message(ext.at[:, pl.ds(tokens, RIM), :], rim, rim, (next_ctx, tp))
    start(rim_m)

    across.recv()
    start_all(xb_m)
    start_all(za_m[1])
    start_all(xa_m[0])

    group_count = rates.shape[0]
    spread = (
        lax.broadcasted_iota(jnp.int32, (group_count, channels), 1) // (channels // group_count)
        == lax.broadcasted_iota(jnp.int32, (group_count, channels), 0)
    ).astype(jnp.float32)
    by_pole = (((0,), (0,)), ((), ()))
    rate = lax.dot_general(rates[...], spread, by_pole, precision=HIGHEST, preferred_element_type=jnp.float32)
    residue = lax.dot_general(residues[...], spread, by_pole, precision=HIGHEST, preferred_element_type=jnp.float32)
    decay[...] = jnp.exp(-rate)
    coef[...] = residue * jnp.sqrt(2.0 * rate) * (1.0 / math.sqrt(poles))
    for k in range(LINE):
        rate_chunks[k] = rate[:, k * LANES : (k + 1) * LANES]

    rim_m.recv()
    has_before = (ctx > 0).astype(jnp.float32)
    for s in range(3):
        ext[s, pl.ds(0, RIM), :] = rim[s] * has_before

    def short(k, carry):
        lanes = pl.ds(pl.multiple_of(k * LANES, LANES), LANES)

        def filtered(s):
            total_ = None
            for shift in range(tap_count):
                term = taps[s, pl.ds(shift, 1), lanes] * ext[s, pl.ds(RIM - shift, tokens), lanes]
                total_ = term if total_ is None else total_ + term
            return total_

        query[:, lanes] = filtered(0)
        gated[:, lanes] = (filtered(1) * filtered(2)).astype(jnp.bfloat16).astype(jnp.float32)
        return carry

    lax.fori_loop(0, channels // LANES, short, 0)

    unroll = 8
    for h in range(2):
        lanes = pl.ds(h * half, half)
        fall = decay[:, lanes]

        def step(t, state):
            for u in range(unroll):
                state = state * fall + gated[pl.ds(t * unroll + u, 1), lanes]
            return state

        state = lax.fori_loop(0, tokens // unroll, step, jnp.zeros((poles, half), jnp.float32))
        for k in range(half // LANES):
            ends[h * (half // LANES) + k] = state[:, k * LANES : (k + 1) * LANES]

    round1 = []
    for m in range(1, LINE):
        to = flip(place, m)
        round1.append(message(ends.at[to], line_in.at[place], line_in.at[to], (ctx - place + to, tp)))
    start_all(round1)
    line_in[place] = ends[place]

    recv_all(xb_m)
    start_all(xbf_m)
    recv_all(za_m[1])
    start_all(za_m[2])
    start_all(xa_m[1])

    recv_all(round1)
    my_rate = rate_chunks[place]
    block_fall = jnp.exp(my_rate * (-float(tokens)))
    row_fall = jnp.exp(my_rate * (-float(tokens * LINE)))
    state = line_in[0]
    for p in range(1, LINE):
        state = state * block_fall + line_in[p]
    row_total[...] = state
    row_in[row] = state

    round2 = []
    for dy in range(2):
        for m in range(NZ):
            if (dy, m) == (0, 0):
                continue
            other = (y + dy) % 2 * NZ + flip(z, m)
            round2.append(message(row_total, row_in.at[row], row_in.at[other], (other * LINE + place, tp)))
    start_all(round2)

    recv_all(xa_m[0])
    start_all(xaf_m[0])
    recv_all(xbf_m)
    start_all(zb_m[1])
    recv_all(za_m[2])
    start_all(za_m[3])
    start_all(xa_m[2])

    recv_all(round2)
    state = jnp.zeros((poles, LANES), jnp.float32)
    for r in range(2 * NZ - 1):
        state = jnp.where(r < row, state * row_fall + row_in[r], state)
    for p in range(LINE):
        enter_out[p] = state
        if p < LINE - 1:
            state = state * block_fall + line_in[p]

    round3 = []
    for m in range(1, LINE):
        to = flip(place, m)
        round3.append(message(enter_out.at[to], enter_in.at[place], enter_in.at[to], (ctx - place + to, tp)))
    start_all(round3)
    enter_in[place] = enter_out[place]

    recv_all(xa_m[1])
    start_all(xaf_m[1])
    recv_all(za_m[3])
    start_all(za_m[4])
    start_all(xa_m[3])

    recv_all(round3)

    right_m, left_m = {}, {}
    right_to, left_to = (ctx, (tp + 1) % tp_n), (ctx, (tp + tp_n - 1) % tp_n)
    for h in range(2):
        for d in range(3):
            behind, ahead = (tp + tp_n - d) % tp_n, (tp + d) % tp_n
            right_m[h, d] = message(
                mixed.at[h, behind], mixed.at[h, behind], mixed.at[h, (tp + tp_n - 1 - d) % tp_n], right_to
            )
            left_m[h, d] = message(
                mixed.at[h, ahead], mixed.at[h, ahead], mixed.at[h, (tp + 1 + d) % tp_n], left_to
            )

    def line_send(h, d):
        @pl.when((tp < tp_n - 1) & (tp >= d))
        def _():
            right_m[h, d].start()

        @pl.when((tp > 0) & (tp + d < tp_n))
        def _():
            left_m[h, d].start()

    def line_sent(h, d):
        @pl.when((tp < tp_n - 1) & (tp >= d))
        def _():
            right_m[h, d].sent()

        @pl.when((tp > 0) & (tp + d < tp_n))
        def _():
            left_m[h, d].sent()

    def line_recv(h, d):
        @pl.when(tp >= d + 1)
        def _():
            right_m[h, d].recv()

        @pl.when(tp + d + 1 < tp_n)
        def _():
            left_m[h, d].recv()

    for h in range(2):
        lanes = pl.ds(h * half, half)
        fall, gain = decay[:, lanes], coef[:, lanes]
        first = h * (half // LANES)
        enter = jnp.concatenate([enter_in[first + k] for k in range(half // LANES)], axis=1)

        def step(t, state):
            for u in range(unroll):
                at_t = pl.ds(t * unroll + u, 1)
                state = state * fall + gated[at_t, lanes]
                conv[at_t, lanes] = jnp.sum(state * gain, axis=0, keepdims=True)
            return state

        lax.fori_loop(0, tokens // unroll, step, enter)
        mixed[h, tp] = (
            query[:, lanes] * (conv[:, lanes] + skip[:, lanes] * gated[:, lanes])
        ).astype(jnp.bfloat16)
        line_send(h, 0)

    recv_all(zb_m[1])
    start_all(zb_m[2])
    start_all(share_m[1, 0])
    start_all(share_m[1, 1])
    recv_all(xa_m[2])
    start_all(xaf_m[2])
    recv_all(za_m[4])
    start_all(xa_m[4])
    for h in range(2):
        line_recv(h, 0)
        line_send(h, 1)
    recv_all(zb_m[2])
    start_all(zb_m[3])
    start_all(share_m[1, 2])
    recv_all(xa_m[3])
    start_all(xaf_m[3])
    recv_all(xa_m[4])
    start_all(xaf_m[4])
    for h in range(2):
        line_recv(h, 1)
        line_send(h, 2)
    recv_all(zb_m[3])
    start_all(zb_m[4])
    start_all(share_m[1, 3])
    for g in range(5):
        recv_all(xaf_m[g])
        start_all(share_m[0, g])
    recv_all(zb_m[4])
    start_all(share_m[1, 4])
    for h in range(2):
        line_recv(h, 2)
    for key in share_m:
        recv_all(share_m[key])

    total[...] = jnp.zeros_like(total)

    def project(k, carry):
        y_, z_ = k // NZ, k % NZ
        behind = (z_ + NZ - z) % NZ
        slot = jnp.where(behind <= 4, jnp.maximum(2 * behind - 1, 0), 2 * (NZ - behind))
        block, rest = k // 4, k % 4
        weights = w[y_, slot].reshape(LINE * rows, w.shape[-1])
        part = pl.ds(pl.multiple_of((rest % 2) * (LINE * rows), LINE * rows), LINE * rows)
        total[...] += jnp.dot(
            mixed[rest // 2, block, :, part], weights, preferred_element_type=jnp.float32
        )
        return carry

    lax.fori_loop(0, 2 * NZ, project, 0)
    out[...] = total[...].astype(jnp.bfloat16)

    for made in sent:
        made.sent()
    for h in range(2):
        for d in range(3):
            line_sent(h, d)


def local(streams, conv_weight, rates, residues, skip, out_weight):
    channels, tokens = streams.shape[1:]
    poles = rates.shape[1]
    rows, features = out_weight.shape
    vmem = pl.BlockSpec(memory_space=pltpu.VMEM)
    f32, bf16 = jnp.float32, jnp.bfloat16
    messages = 1 + 8 + 20 + 4 + 8 + 10 + 1 + 7 + 15 + 7 + 12
    return pl.pallas_call(
        functools.partial(kernel, conv_weight.shape[1]),
        out_shape=jax.ShapeDtypeStruct((tokens, features), bf16),
        in_specs=[vmem] * 6,
        out_specs=vmem,
        scratch_shapes=[
            pltpu.VMEM((2, NZ, NX, 2, rows, features), bf16),
            pltpu.VMEM((3, RIM + tokens, channels), f32),
            pltpu.VMEM((3, RIM, channels), f32),
            pltpu.VMEM((tokens, channels), f32),
            pltpu.VMEM((tokens, channels), f32),
            pltpu.VMEM((tokens, channels), f32),
            pltpu.VMEM((poles, channels), f32),
            pltpu.VMEM((poles, channels), f32),
            pltpu.VMEM((LINE, poles, LANES), f32),
            pltpu.VMEM((LINE, poles, LANES), f32),
            pltpu.VMEM((LINE, poles, LANES), f32),
            pltpu.VMEM((poles, LANES), f32),
            pltpu.VMEM((2 * NZ, poles, LANES), f32),
            pltpu.VMEM((LINE, poles, LANES), f32),
            pltpu.VMEM((LINE, poles, LANES), f32),
            pltpu.VMEM((2, 4, tokens, channels // 2), bf16),
            pltpu.VMEM((tokens, features), f32),
            pltpu.SemaphoreType.DMA((messages,)),
            pltpu.SemaphoreType.DMA((messages,)),
        ],
        compiler_params=pltpu.CompilerParams(
            collective_id=0, has_side_effects=True, vmem_limit_bytes=48 * 1024 * 1024
        ),
        cost_estimate=pl.CostEstimate(
            flops=2 * tokens * 4 * channels * features, bytes_accessed=12 << 20, transcendentals=1 << 15
        ),
    )(streams, conv_weight, rates, residues, skip.reshape(1, channels), out_weight)


def solution(mesh):
    return jax.shard_map(
        local,
        mesh=mesh,
        in_specs=(
            P(None, "tp", "ctx"),
            P(None, None, "tp"),
            P("tp", None),
            P("tp", None),
            P("tp"),
            P("ctx", "tp"),
        ),
        out_specs=P("ctx", "tp"),
        check_vma=False,
    )
```

time: 294 us -> 78.3 us (0.27)
  waiting for transfers between devices: 208 us -> 0 us
  Pallas kernels: 0 us -> 73.7 us
  blocking collectives: 29.5 us -> 0 us
  starting transfers between devices: 22.8 us -> 0 us
  between operations: 13.6 us -> 0.04 us
  matrix products: 9.69 us -> 0 us
  other arithmetic: 7.52 us -> 0 us
    all_gather x2 -> x0, waiting for transfers between devices: 186 us -> none  [the longest x1 160 us: local(): lax.all_gather(out_weight, 'ctx', axis=0, tiled=True)]
    pallas_call x0 -> x1, Pallas kernels: none -> 73.7 us  [local(): pl.pallas_call(functools.partial(kernel, conv_weight.shape[1]), out_shape...]
    all_to_all x1 -> x0, blocking collectives: 29.5 us -> none  [local(): lax.all_to_all(filtered_all, 'ctx', split_axis=1, concat_axis=0, tiled=True)]
    all_to_all x1 -> x0, starting transfers between devices: 18.2 us -> none  [local(): lax.all_to_all(gated_in, 'ctx', split_axis=0, concat_axis=1, tiled=True)]
    all_to_all x1 -> x0, waiting for transfers between devices: 17 us -> none  [local(): lax.all_to_all(gated_in, 'ctx', split_axis=0, concat_axis=1, tiled=True)]
    dot_general x6 -> x0, matrix products: 9.69 us -> none  [the longest x1 5.7 us: local(): lax.dot_general(features, lax.all_gather(out_weight, 'ctx', axis=0, tiled...]
    add x2 -> x0, other arithmetic: 5.58 us -> none  [the longest x1 5.58 us: local(): filtered + conv_weight[:, shift_by, :, None] * extended[:, :, rim_width -...]
    ppermute x1 -> x0, starting transfers between devices: 4.51 us -> none  [from_behind(): lax.ppermute(value, axis, [(source, source + steps) for source in range(l...]
  transfers between devices with their start and end apart: 4 -> 0, of which waited for: 4 -> 0; matrix products, arithmetic and copies ran while one was open for 0% -> 0% of each run, Pallas kernels for 0% -> 0%
where the time goes in v1:
time: 78.3 us; the launch traced here: 78 us
  Pallas kernels  73.7 us (94%)
  local copies, waits for them, and re-layouts  4.31 us (6%)
    pallas_call x1, Pallas kernels, local(): pl.pallas_call(functools.partial(kernel, conv_weight.shape[1]), out_shape...  73.7 us
    unnamed x11, local copies, waits for them, and re-layouts  4.31 us

profile of v1, /device:TPU:1, one launch (start us, length us, event | category | flops | bytes accessed | tf_op | source)
XLA Modules:
  0.0 78.0 jit_solution(2435641925461859394)
XLA Ops:
  0.0 0.0 copy-start.1
  0.0 0.8 %copy.7.rates = f32[128,16]{1,0:T(8,128)S(1)} copy(f32[128,16]{0,1:T(8,128)} %param.8) | data formatting | bytes 16384 | tf_op args[2]
  0.8 0.0 copy-start.3
  0.8 0.8 %copy.8.residues = f32[128,16]{1,0:T(8,128)S(1)} copy(f32[128,16]{0,1:T(8,128)} %param.9) | data formatting | bytes 16384 | tf_op args[3]
  1.6 0.0 copy-done.1
  1.7 0.0 copy-done.3
  1.7 0.0 copy-start
  1.7 1.1 %copy-done = bf16[3,1024,128]{2,1,0:T(8,128)(2,1)S(1)} copy-done((bf16[3,1024,128]{2,1,0:T(8,128)(2,1)S(1)}, bf16[3,1024,128]{2,1,0:T(8,128)(2,1)}, u32[]{:S(2)}) %copy-start) | copy-done | bytes 786456
  2.8 0.0 copy-start.2
  2.8 0.8 %copy-done.2 = bf16[32,1024]{1,0:T(8,128)(2,1)S(1)} copy-done((bf16[32,1024]{1,0:T(8,128)(2,1)S(1)}, bf16[32,1024]{1,0:T(8,128)(2,1)}, u32[]{:S(2)}) %copy-start.2) | copy-done | bytes 65560
  3.6 73.7 %shard_map.64 = bf16[128,1024]{1,0:T(8,128)(2,1)S(1)} custom-call(bf16[3,1024,128]{2,1,0:T(8,128)(2,1)S(1)} %copy-done, f32[3,7,1024]{2,1,0:T(8,128)S(1)} %copy-done.1, f32[128,16]{1,0:T(8,128)S(1)} %copy.7.rates, f32[128,16]{1,0:T(8,128)S(1)} %copy.8.residues, f32[1,1024]{1,0:T(1,128)S(1)} %bitcast.1, bf16[32,1024]{1,0:T(8,128)(2,1)S(1)} %copy-done.2), custom_call_target="tpu_custom_call" | custom-call | flops 1073741824 | bytes 12582912 | tf_op jit(solution)/shard_map/pallas_call | solution.py:468
  77.3 0.7 copy.10
Async XLA Ops:
  0.0 1.6 %copy-start.1 = (f32[3,7,1024]{2,1,0:T(8,128)S(1)}, f32[3,7,1024]{2,1,0:T(8,128)}, u32[]{:S(2)}) copy-start(f32[3,7,1024]{2,1,0:T(8,128)} %taps.1) | copy-start | bytes 258052
  0.8 0.8 %copy-start.3 = (f32[1024]{0:T(1024)S(1)}, f32[1024]{0:T(1024)}, u32[]{:S(2)}) copy-start(f32[1024]{0:T(1024)} %param.10) | copy-start | bytes 12292
  1.7 1.1 %copy-start = (bf16[3,1024,128]{2,1,0:T(8,128)(2,1)S(1)}, bf16[3,1024,128]{2,1,0:T(8,128)(2,1)}, u32[]{:S(2)}) copy-start(bf16[3,1024,128]{2,1,0:T(8,128)(2,1)} %streams.1) | copy-start | bytes 2359300
  2.8 0.8 %copy-start.2 = (bf16[32,1024]{1,0:T(8,128)(2,1)S(1)}, bf16[32,1024]{1,0:T(8,128)(2,1)}, u32[]{:S(2)}) copy-start(bf16[32,1024]{1,0:T(8,128)(2,1)} %w_in.1) | copy-start | bytes 196612

commit v2 on v1

v2 whole, which is shorter than its diff:
```python
import functools
import math

import jax
import jax.numpy as jnp
from jax import lax
from jax.experimental import pallas as pl
from jax.experimental.pallas import tpu as pltpu
from jax.sharding import PartitionSpec as P

NZ, NX = 8, 4
LINE = NX * 2
LANES = 128
RIM = 8
HIGHEST = lax.Precision.HIGHEST


class Message:
    def __init__(self, sems, number, src, dst, land, to):
        send, recv = sems
        make = functools.partial(
            pltpu.make_async_remote_copy,
            send_sem=send.at[number],
            recv_sem=recv.at[number],
            device_id=to,
            device_id_type=pl.DeviceIdType.MESH,
        )
        self.out = make(src_ref=src, dst_ref=dst)
        self.into = make(src_ref=src, dst_ref=land)

    def start(self):
        self.out.start()

    def recv(self):
        self.into.wait_recv()

    def sent(self):
        self.out.wait_send()


def kernel(
    tap_count,
    streams_hbm,
    taps_hbm,
    rates_hbm,
    residues_hbm,
    skip_hbm,
    w_hbm,
    out,
    w,
    streams,
    taps,
    rates,
    residues,
    skip,
    ext,
    query,
    gated,
    conv,
    decay,
    coef,
    rate_chunks,
    ends,
    line_in,
    row_total,
    row_in,
    part_total,
    part_in,
    enter_out,
    enter_in,
    mixed,
    total,
    load_sems,
    send_sems,
    recv_sems,
):
    poles = rates.shape[0]
    channels, tokens = streams.shape[1:]
    half = channels // 2
    rows = w_hbm.shape[0]
    ctx, tp = lax.axis_index("ctx"), lax.axis_index("tp")
    ctx_n, tp_n = lax.axis_size("ctx"), lax.axis_size("tp")
    core = ctx % 2
    x = (ctx // 2) % NX
    z = (ctx // LINE) % NZ
    y = ctx // (LINE * NZ)
    place = ctx % LINE

    def at(y_=None, z_=None, x_=None, core_=None):
        y_ = y if y_ is None else y_
        z_ = z if z_ is None else z_
        x_ = x if x_ is None else x_
        core_ = core if core_ is None else core_
        return (((y_ * NZ + z_) * NX + x_) * 2 + core_, tp)

    def flip(value, bits):
        result = value * 0
        for bit in (1, 2, 4):
            digit = (value // bit) % 2
            result = result + bit * ((1 - digit) if bits & bit else digit)
        return result

    sems = (send_sems, recv_sems)
    count = [0]
    sent = []

    def message(src, dst, land, to):
        made = Message(sems, count[0], src, dst, land, to)
        count[0] += 1
        return made

    def start_all(pair):
        for made in pair:
            made.start()
            sent.append(made)

    def recv_all(pair):
        for made in pair:
            made.recv()

    barrier = pltpu.get_barrier_semaphore()

    def greet(peer):
        pl.semaphore_signal(barrier, inc=1, device_id=peer, device_id_type=pl.DeviceIdType.MESH)

    always = [at(y_=1 - y)]
    always += [(ctx - place + flip(place, m), tp) for m in range(1, LINE)]
    always += [at(z_=flip(z, m)) for m in range(1, NZ)]
    sometimes = [
        (ctx < ctx_n - 1, (ctx + 1, tp)),
        (ctx > 0, (ctx - 1, tp)),
        (tp < tp_n - 1, (ctx, tp + 1)),
        (tp > 0, (ctx, tp - 1)),
    ]
    greetings = len(always)
    for peer in always:
        greet(peer)
    for there, peer in sometimes:
        pl.when(there)(functools.partial(greet, peer))
        greetings = greetings + there.astype(jnp.int32)

    loads = [
        pltpu.make_async_copy(src, dst, load_sems.at[n])
        for n, (src, dst) in enumerate(
            [
                (w_hbm, w.at[y, 0, x, core]),
                (streams_hbm, streams),
                (rates_hbm, rates),
                (residues_hbm, residues),
                (taps_hbm, taps),
                (skip_hbm, skip),
            ]
        )
    ]
    for load in loads:
        load.start()

    groups = [(0, 1), (1, 2), (3, 2), (5, 2), (7, 1)]
    ups, downs = at(z_=(z + 1) % NZ), at(z_=(z + NZ - 1) % NZ)
    rights, lefts = at(x_=(x + 1) % NX), at(x_=(x + NX - 1) % NX)
    x_left, x_right = (x + NX - 1) % NX, (x + 1) % NX
    x_far = (x + 2) % NX
    sibling = at(core_=1 - core)
    top, bottom = pl.ds(0, rows // 2), pl.ds(rows // 2, rows // 2)
    own, other = y, 1 - y

    across = (message(w.at[own, 0, x, core], w.at[own, 0, x, core], w.at[other, 0, x, core], at(y_=other)),)

    def za(step):
        up_src, down_src = max(2 * step - 2, 0), max(2 * step - 3, 0)
        if step < 4:
            up_dst, down_dst = w.at[other, 2 * step, x, core], w.at[other, 2 * step - 1, x, core]
            return (
                message(w.at[other, up_src, x, core], up_dst, up_dst, ups),
                message(w.at[other, down_src, x, core], down_dst, down_dst, downs),
            )
        up_dst, down_dst = w.at[other, 7, x, core, top], w.at[other, 7, x, core, bottom]
        return (
            message(w.at[other, 6, x, core, top], up_dst, up_dst, ups),
            message(w.at[other, 5, x, core, bottom], down_dst, down_dst, downs),
        )

    def xa(y_, group):
        slots = pl.ds(*groups[group])
        mine = w.at[y_, slots, x, core]
        return (
            message(mine, mine, w.at[y_, slots, x_left, core], rights),
            message(mine, mine, w.at[y_, slots, x_right, core], lefts),
        )

    def xa_far(y_, group):
        slots = pl.ds(*groups[group])
        from_left = w.at[y_, slots, x_left, core, top]
        from_right = w.at[y_, slots, x_right, core, bottom]
        return (
            message(from_left, from_left, w.at[y_, slots, x_far, core, top], rights),
            message(from_right, from_right, w.at[y_, slots, x_far, core, bottom], lefts),
        )

    def zb(step):
        up_src, down_src = max(2 * step - 2, 0), max(2 * step - 3, 0)
        if step < 4:
            every = pl.ds(0, NX)
            up_dst, down_dst = w.at[own, 2 * step, every, core], w.at[own, 2 * step - 1, every, core]
            return (
                message(w.at[own, up_src, every, core], up_dst, up_dst, ups),
                message(w.at[own, down_src, every, core], down_dst, down_dst, downs),
            )
        first, second = pl.ds(0, NX // 2), pl.ds(NX // 2, NX // 2)
        up_dst, down_dst = w.at[own, 7, first, core], w.at[own, 7, second, core]
        return (
            message(w.at[own, 6, first, core], up_dst, up_dst, ups),
            message(w.at[own, 5, second, core], down_dst, down_dst, downs),
        )

    def share(y_, group):
        slots = pl.ds(*groups[group])
        mine = w.at[y_, slots, pl.ds(0, NX), core]
        return (message(mine, mine, w.at[y_, slots, pl.ds(0, NX), 1 - core], sibling),)

    za_m = {s: za(s) for s in (1, 2, 3, 4)}
    xa_m = {g: xa(other, g) for g in range(5)}
    xaf_m = {g: xa_far(other, g) for g in range(5)}
    xb_m, xbf_m = xa(own, 0), xa_far(own, 0)
    zb_m = {s: zb(s) for s in (1, 2, 3, 4)}
    own_share = {g: share(own, g) for g in range(5)}
    other_share = {g: share(other, g) for g in range(5)}

    rim_m = message(ext.at[:, pl.ds(tokens, RIM), :], ext.at[:, pl.ds(0, RIM), :], ext.at[:, pl.ds(0, RIM), :], (ctx + 1, tp))
    eye = (
        lax.broadcasted_iota(jnp.int32, (tokens, tokens), 0)
        == lax.broadcasted_iota(jnp.int32, (tokens, tokens), 1)
    ).astype(jnp.bfloat16)
    loads[0].wait()
    loads[1].wait()
    for s in range(3):
        ext[s, pl.ds(RIM, tokens), :] = lax.dot_general(
            eye, streams[s], (((1,), (1,)), ((), ())), preferred_element_type=jnp.float32
        )
    pl.semaphore_wait(barrier, greetings)

    pl.when(ctx < ctx_n - 1)(rim_m.start)
    start_all(across)
    start_all(xb_m)

    for load in loads[2:]:
        load.wait()
    group_count = rates.shape[1]
    spread = (
        lax.broadcasted_iota(jnp.int32, (group_count, channels), 1) // (channels // group_count)
        == lax.broadcasted_iota(jnp.int32, (group_count, channels), 0)
    ).astype(jnp.float32)
    plain = (((1,), (0,)), ((), ()))
    rate = lax.dot_general(rates[...], spread, plain, precision=HIGHEST, preferred_element_type=jnp.float32)
    residue = lax.dot_general(residues[...], spread, plain, precision=HIGHEST, preferred_element_type=jnp.float32)
    decay[...] = jnp.exp(-rate)
    coef[...] = residue * jnp.sqrt(2.0 * rate) * (1.0 / math.sqrt(poles))
    for k in range(LINE):
        rate_chunks[k] = rate[:, k * LANES : (k + 1) * LANES]

    def short_rows(first, length):
        def short(k, carry):
            lanes = pl.ds(pl.multiple_of(k * LANES, LANES), LANES)

            def filtered(s):
                total_ = None
                for shift in range(tap_count):
                    term = taps[s, pl.ds(shift, 1), lanes] * ext[s, pl.ds(RIM + first - shift, length), lanes]
                    total_ = term if total_ is None else total_ + term
                return total_

            at_rows = pl.ds(first, length)
            query[at_rows, lanes] = filtered(0)
            gated[at_rows, lanes] = (filtered(1) * filtered(2)).astype(jnp.bfloat16).astype(jnp.float32)
            return carry

        lax.fori_loop(0, channels // LANES, short, 0)

    unroll = 8

    def run_states(first, length, lanes, state):
        fall = decay[:, lanes]

        def step(t, state):
            for u in range(unroll):
                state = state * fall + gated[pl.ds(first + t * unroll + u, 1), lanes]
            return state

        return lax.fori_loop(0, length // unroll, step, state)

    short_rows(RIM, tokens - RIM)
    halves = [pl.ds(h * half, half) for h in range(2)]
    zeros = jnp.zeros((poles, half), jnp.float32)
    for h in range(2):
        state = run_states(RIM, tokens - RIM, halves[h], zeros)
        for k in range(half // LANES):
            ends[h * (half // LANES) + k] = state[:, k * LANES : (k + 1) * LANES]

    @pl.when(ctx > 0)
    def _():
        rim_m.recv()

    @pl.when(ctx == 0)
    def _():
        for s in range(3):
            ext[s, pl.ds(0, RIM), :] = jnp.zeros((RIM, channels), jnp.float32)

    short_rows(0, RIM)
    for h in range(2):
        state = run_states(0, RIM, halves[h], zeros)
        for k in range(half // LANES):
            n = h * (half // LANES) + k
            ends[n] += state[:, k * LANES : (k + 1) * LANES] * jnp.exp(rate_chunks[n] * (-float(tokens - RIM)))

    round1 = []
    for m in range(1, LINE):
        to = flip(place, m)
        round1.append(message(ends.at[to], line_in.at[place], line_in.at[to], (ctx - place + to, tp)))
    start_all(round1)
    line_in[place] = ends[place]

    recv_all(xb_m)
    start_all(xbf_m)

    recv_all(round1)
    my_rate = rate_chunks[place]
    block_fall = jnp.exp(my_rate * (-float(tokens)))
    row_fall = jnp.exp(my_rate * (-float(tokens * LINE)))
    state = line_in[0]
    for p in range(1, LINE):
        state = state * block_fall + line_in[p]
    row_total[...] = state
    row_in[z] = state

    round2 = []
    for m in range(1, NZ):
        to = flip(z, m)
        round2.append(message(row_total, row_in.at[z], row_in.at[to], at(z_=to)))
    start_all(round2)

    recv_all(xbf_m)
    start_all(zb_m[1])
    recv_all(across)
    start_all(za_m[1])
    start_all(xa_m[0])

    recv_all(round2)
    onward = message(part_total, part_in, part_in, at(y_=1 - y))

    @pl.when(y == 0)
    def _():
        state = row_in[0]
        for r in range(1, NZ):
            state = state * row_fall + row_in[r]
        part_total[...] = state
        onward.start()
        part_in[...] = jnp.zeros_like(part_in)

    recv_all(za_m[1])
    start_all(za_m[2])
    start_all(xa_m[1])
    recv_all(xa_m[0])
    start_all(xaf_m[0])

    @pl.when(y == 1)
    def _():
        onward.recv()

    state = part_in[...]
    for r in range(NZ - 1):
        state = jnp.where(r < z, state * row_fall + row_in[r], state)
    for p in range(LINE):
        enter_out[p] = state
        if p < LINE - 1:
            state = state * block_fall + line_in[p]

    round3 = []
    for m in range(1, LINE):
        to = flip(place, m)
        round3.append(message(enter_out.at[to], enter_in.at[place], enter_in.at[to], (ctx - place + to, tp)))
    start_all(round3)
    enter_in[place] = enter_out[place]

    recv_all(za_m[2])
    start_all(za_m[3])
    start_all(xa_m[2])
    recv_all(xa_m[1])
    start_all(xaf_m[1])

    recv_all(round3)

    right_m, left_m = {}, {}
    for h in range(2):
        for d in range(3):
            behind, ahead = (tp + tp_n - d) % tp_n, (tp + d) % tp_n
            right_m[h, d] = message(
                mixed.at[h, behind], mixed.at[h, behind], mixed.at[h, (tp + tp_n - 1 - d) % tp_n], (ctx, (tp + 1) % tp_n)
            )
            left_m[h, d] = message(
                mixed.at[h, ahead], mixed.at[h, ahead], mixed.at[h, (tp + 1 + d) % tp_n], (ctx, (tp + tp_n - 1) % tp_n)
            )

    def line_send(h, d):
        pl.when((tp < tp_n - 1) & (tp >= d))(right_m[h, d].start)
        pl.when((tp > 0) & (tp + d < tp_n))(left_m[h, d].start)

    def line_sent(h, d):
        pl.when((tp < tp_n - 1) & (tp >= d))(right_m[h, d].sent)
        pl.when((tp > 0) & (tp + d < tp_n))(left_m[h, d].sent)

    def line_recv(h, d):
        pl.when(tp >= d + 1)(right_m[h, d].recv)
        pl.when(tp + d + 1 < tp_n)(left_m[h, d].recv)

    for h in range(2):
        lanes = halves[h]
        fall, gain = decay[:, lanes], coef[:, lanes]
        first = h * (half // LANES)
        enter = jnp.concatenate([enter_in[first + k] for k in range(half // LANES)], axis=1)

        def step(t, state):
            for u in range(unroll):
                at_t = pl.ds(t * unroll + u, 1)
                state = state * fall + gated[at_t, lanes]
                conv[at_t, lanes] = jnp.sum(state * gain, axis=0, keepdims=True)
            return state

        lax.fori_loop(0, tokens // unroll, step, enter)
        mixed[h, tp] = (
            query[:, lanes] * (conv[:, lanes] + skip[:, lanes] * gated[:, lanes])
        ).astype(jnp.bfloat16)
        line_send(h, 0)

    recv_all(zb_m[1])
    start_all(zb_m[2])
    start_all(own_share[0])
    start_all(own_share[1])
    recv_all(za_m[3])
    start_all(za_m[4])
    start_all(xa_m[3])
    recv_all(xa_m[2])
    start_all(xaf_m[2])
    line_recv(0, 0)
    line_send(0, 1)
    recv_all(za_m[4])
    start_all(xa_m[4])
    line_recv(1, 0)
    line_send(1, 1)
    recv_all(zb_m[2])
    start_all(zb_m[3])
    start_all(own_share[2])
    recv_all(xa_m[3])
    start_all(xaf_m[3])
    line_recv(0, 1)
    line_send(0, 2)
    recv_all(xa_m[4])
    start_all(xaf_m[4])
    line_recv(1, 1)
    line_send(1, 2)
    recv_all(zb_m[3])
    start_all(zb_m[4])
    start_all(own_share[3])
    for g in range(5):
        recv_all(xaf_m[g])
        start_all(other_share[g])
    recv_all(zb_m[4])
    start_all(own_share[4])
    for g in range(5):
        recv_all(own_share[g])
        recv_all(other_share[g])

    deep = LINE * rows

    def project(h, block):
        def step(k, carry):
            place_ = block * 4 + h * 2 + k
            y_, z_ = place_ // NZ, place_ % NZ
            behind = (z_ + NZ - z) % NZ
            slot = jnp.where(behind <= 4, jnp.maximum(2 * behind - 1, 0), 2 * (NZ - behind))
            weights = w[y_, slot].reshape(deep, w.shape[-1])
            part = pl.ds(pl.multiple_of(k * deep, deep), deep)
            total[...] += jnp.dot(mixed[h, block, :, part], weights, preferred_element_type=jnp.float32)
            return carry

        lax.fori_loop(0, 2, step, 0)

    total[...] = jnp.zeros_like(total)
    for h in range(2):
        project(h, tp)
    for d in range(3):
        for h in range(2):
            if d == 2:
                line_recv(h, d)

            @pl.when(tp >= d + 1)
            def _():
                project(h, tp - 1 - d)

            @pl.when(tp + d + 1 < tp_n)
            def _():
                project(h, tp + 1 + d)

    out[...] = total[...].astype(jnp.bfloat16)

    for made in sent:
        made.sent()
    pl.when(ctx < ctx_n - 1)(rim_m.sent)
    pl.when(y == 0)(onward.sent)
    for h in range(2):
        for d in range(3):
            line_sent(h, d)


def local(streams, conv_weight, rates, residues, skip, out_weight):
    channels, tokens = streams.shape[1:]
    groups, poles = rates.shape
    rows, features = out_weight.shape
    anywhere = pl.BlockSpec(memory_space=pl.ANY)
    f32, bf16 = jnp.float32, jnp.bfloat16
    messages = 1 + 8 + 20 + 4 + 8 + 10 + 1 + 7 + 7 + 1 + 7 + 12
    return pl.pallas_call(
        functools.partial(kernel, conv_weight.shape[1]),
        out_shape=jax.ShapeDtypeStruct((tokens, features), bf16),
        in_specs=[anywhere] * 6,
        out_specs=pl.BlockSpec(memory_space=pltpu.VMEM),
        scratch_shapes=[
            pltpu.VMEM((2, NZ, NX, 2, rows, features), bf16),
            pltpu.VMEM(streams.shape, bf16),
            pltpu.VMEM(conv_weight.shape, f32),
            pltpu.VMEM((poles, groups), f32),
            pltpu.VMEM((poles, groups), f32),
            pltpu.VMEM((1, channels), f32),
            pltpu.VMEM((3, RIM + tokens, channels), f32),
            pltpu.VMEM((tokens, channels), f32),
            pltpu.VMEM((tokens, channels), f32),
            pltpu.VMEM((tokens, channels), f32),
            pltpu.VMEM((poles, channels), f32),
            pltpu.VMEM((poles, channels), f32),
            pltpu.VMEM((LINE, poles, LANES), f32),
            pltpu.VMEM((LINE, poles, LANES), f32),
            pltpu.VMEM((LINE, poles, LANES), f32),
            pltpu.VMEM((poles, LANES), f32),
            pltpu.VMEM((NZ, poles, LANES), f32),
            pltpu.VMEM((poles, LANES), f32),
            pltpu.VMEM((poles, LANES), f32),
            pltpu.VMEM((LINE, poles, LANES), f32),
            pltpu.VMEM((LINE, poles, LANES), f32),
            pltpu.VMEM((2, 4, tokens, channels // 2), bf16),
            pltpu.VMEM((tokens, features), f32),
            pltpu.SemaphoreType.DMA((6,)),
            pltpu.SemaphoreType.DMA((messages,)),
            pltpu.SemaphoreType.DMA((messages,)),
        ],
        compiler_params=pltpu.CompilerParams(
            collective_id=0, has_side_effects=True, vmem_limit_bytes=60 * 1024 * 1024
        ),
        cost_estimate=pl.CostEstimate(
            flops=2 * tokens * 4 * channels * features, bytes_accessed=12 << 20, transcendentals=1 << 15
        ),
    )(streams, conv_weight, rates.T, residues.T, skip.reshape(1, channels), out_weight)


def solution(mesh):
    return jax.shard_map(
        local,
        mesh=mesh,
        in_specs=(
            P(None, "tp", "ctx"),
            P(None, None, "tp"),
            P("tp", None),
            P("tp", None),
            P("tp"),
            P("ctx", "tp"),
        ),
        out_specs=P("ctx", "tp"),
        check_vma=False,
    )
```

time: 78.3 us -> 77.5 us (0.990)
  the two profiles are of different devices: /device:TPU:1 before, /device:TPU:41 now
where the time goes in v2:
time: 77.5 us; the launch traced here: 77.3 us
  Pallas kernels  75.6 us (98%)
  local copies, waits for them, and re-layouts  1.67 us (2%)
    pallas_call x1, Pallas kernels, local(): pl.pallas_call(functools.partial(kernel, conv_weight.shape[1]), out_shape...  75.6 us
    unnamed x1, local copies, waits for them, and re-layouts  1.67 us

profile of v2, /device:TPU:41, one launch (start us, length us, event | category | flops | bytes accessed | tf_op | source)
XLA Modules:
  0.0 77.3 jit_solution(6408501570818220151)
XLA Ops:
  0.0 75.6 %shard_map.64 = bf16[128,1024]{1,0:T(8,128)(2,1)} custom-call(bf16[3,1024,128]{2,1,0:T(8,128)(2,1)} %streams_hbm.1, f32[3,7,1024]{2,1,0:T(8,128)} %taps_hbm.1, f32[16,128]{1,0:T(8,128)} %bitcast.3, f32[16,128]{1,0:T(8,128)} %bitcast.4, f32[1,1024]{1,0:T(1,128)} %bitcast.5, bf16[32,1024]{1,0:T(8,128)(2,1)} %w_hbm.1), custom_call_target="tpu_custom_call" | custom-call | flops 1073741824 | bytes 12582912 | tf_op jit(solution)/shard_map/pallas_call | solution.py:521
  75.6 1.7 %copy.8 = bf16[128,1024]{1,0:T(8,128)(2,1)} copy(bf16[128,1024]{1,0:T(8,128)(2,1)} %shard_map.64) | data formatting | bytes 524288

commit v3 on v2

--- a/solution.py
+++ b/solution.py
@@ -197,21 +197,17 @@
             message(from_right, from_right, w.at[y_, slots, x_far, core, bottom], lefts),
         )
 
-    def zb(step):
+    def zb(step, x_, far_up):
         up_src, down_src = max(2 * step - 2, 0), max(2 * step - 3, 0)
-        if step < 4:
-            every = pl.ds(0, NX)
-            up_dst, down_dst = w.at[own, 2 * step, every, core], w.at[own, 2 * step - 1, every, core]
-            return (
-                message(w.at[own, up_src, every, core], up_dst, up_dst, ups),
-                message(w.at[own, down_src, every, core], down_dst, down_dst, downs),
-            )
-        first, second = pl.ds(0, NX // 2), pl.ds(NX // 2, NX // 2)
-        up_dst, down_dst = w.at[own, 7, first, core], w.at[own, 7, second, core]
-        return (
-            message(w.at[own, 6, first, core], up_dst, up_dst, ups),
-            message(w.at[own, 5, second, core], down_dst, down_dst, downs),
-        )
+        up_dst, down_dst = min(2 * step, 7), 2 * step - 1
+        pair = ()
+        if step < 4 or far_up:
+            dst = w.at[own, up_dst, x_, core]
+            pair += (message(w.at[own, up_src, x_, core], dst, dst, ups),)
+        if step < 4 or not far_up:
+            dst = w.at[own, down_dst, x_, core]
+            pair += (message(w.at[own, down_src, x_, core], dst, dst, downs),)
+        return pair
 
     def share(y_, group):
         slots = pl.ds(*groups[group])
@@ -222,9 +218,14 @@
     xa_m = {g: xa(other, g) for g in range(5)}
     xaf_m = {g: xa_far(other, g) for g in range(5)}
     xb_m, xbf_m = xa(own, 0), xa_far(own, 0)
-    zb_m = {s: zb(s) for s in (1, 2, 3, 4)}
+    chains = {"mine": (x, True), "left": (x_left, True), "right": (x_right, False), "far": (x_far, False)}
+    zb_m = {(c, s): zb(s, *chains[c]) for c in chains for s in (1, 2, 3, 4)}
     own_share = {g: share(own, g) for g in range(5)}
     other_share = {g: share(other, g) for g in range(5)}
+
+    def zb_next(chain, step):
+        recv_all(zb_m[chain, step])
+        start_all(zb_m[chain, step + 1])
 
     rim_m = message(ext.at[:, pl.ds(tokens, RIM), :], ext.at[:, pl.ds(0, RIM), :], ext.at[:, pl.ds(0, RIM), :], (ctx + 1, tp))
     eye = (
@@ -240,8 +241,9 @@
     pl.semaphore_wait(barrier, greetings)
 
     pl.when(ctx < ctx_n - 1)(rim_m.start)
+    start_all(xb_m)
+    start_all(zb_m["mine", 1])
     start_all(across)
-    start_all(xb_m)
 
     for load in loads[2:]:
         load.wait()
@@ -321,6 +323,9 @@
 
     recv_all(xb_m)
     start_all(xbf_m)
+    start_all(zb_m["left", 1])
+    start_all(zb_m["right", 1])
+    zb_next("mine", 1)
 
     recv_all(round1)
     my_rate = rate_chunks[place]
@@ -339,10 +344,11 @@
     start_all(round2)
 
     recv_all(xbf_m)
-    start_all(zb_m[1])
+    start_all(zb_m["far", 1])
     recv_all(across)
     start_all(za_m[1])
     start_all(xa_m[0])
+    zb_next("mine", 2)
 
     recv_all(round2)
     onward = message(part_total, part_in, part_in, at(y_=1 - y))
@@ -356,11 +362,14 @@
         onward.start()
         part_in[...] = jnp.zeros_like(part_in)
 
+    zb_next("left", 1)
+    zb_next("right", 1)
     recv_all(za_m[1])
     start_all(za_m[2])
     start_all(xa_m[1])
     recv_all(xa_m[0])
     start_all(xaf_m[0])
+    zb_next("far", 1)
 
     @pl.when(y == 1)
     def _():
@@ -384,6 +393,9 @@
     recv_all(za_m[2])
     start_all(za_m[3])
     start_all(xa_m[2])
+    zb_next("mine", 3)
+    zb_next("left", 2)
+    zb_next("right", 2)
     recv_all(xa_m[1])
     start_all(xaf_m[1])
 
@@ -431,40 +443,42 @@
         ).astype(jnp.bfloat16)
         line_send(h, 0)
 
-    recv_all(zb_m[1])
-    start_all(zb_m[2])
-    start_all(own_share[0])
-    start_all(own_share[1])
     recv_all(za_m[3])
     start_all(za_m[4])
     start_all(xa_m[3])
+    zb_next("far", 2)
+    zb_next("left", 3)
+    zb_next("right", 3)
     recv_all(xa_m[2])
     start_all(xaf_m[2])
+    start_all(own_share[0])
+    start_all(own_share[1])
+    start_all(own_share[2])
     line_recv(0, 0)
     line_send(0, 1)
     recv_all(za_m[4])
     start_all(xa_m[4])
+    zb_next("far", 3)
+    start_all(own_share[3])
     line_recv(1, 0)
     line_send(1, 1)
-    recv_all(zb_m[2])
-    start_all(zb_m[3])
-    start_all(own_share[2])
     recv_all(xa_m[3])
     start_all(xaf_m[3])
+    for g in range(3):
+        recv_all(xaf_m[g])
+        start_all(other_share[g])
     line_recv(0, 1)
     line_send(0, 2)
     recv_all(xa_m[4])
     start_all(xaf_m[4])
+    for c in chains:
+        recv_all(zb_m[c, 4])
+    start_all(own_share[4])
     line_recv(1, 1)
     line_send(1, 2)
-    recv_all(zb_m[3])
-    start_all(zb_m[4])
-    start_all(own_share[3])
-    for g in range(5):
+    for g in range(3, 5):
         recv_all(xaf_m[g])
         start_all(other_share[g])
-    recv_all(zb_m[4])
-    start_all(own_share[4])
     for g in range(5):
         recv_all(own_share[g])
         recv_all(other_share[g])
@@ -517,7 +531,7 @@
     rows, features = out_weight.shape
     anywhere = pl.BlockSpec(memory_space=pl.ANY)
     f32, bf16 = jnp.float32, jnp.bfloat16
-    messages = 1 + 8 + 20 + 4 + 8 + 10 + 1 + 7 + 7 + 1 + 7 + 12
+    messages = 1 + 8 + 20 + 4 + 28 + 10 + 1 + 7 + 7 + 1 + 7 + 12
     return pl.pallas_call(
         functools.partial(kernel, conv_weight.shape[1]),
         out_shape=jax.ShapeDtypeStruct((tokens, features), bf16),

time: 77.5 us -> 65.4 us (0.84)
  the two profiles are of different devices: /device:TPU:41 before, /device:TPU:1 now
where the time goes in v3:
time: 65.4 us; the launch traced here: 64.3 us
  Pallas kernels  62.7 us (96%)
  local copies, waits for them, and re-layouts  1.67 us (3%)
    pallas_call x1, Pallas kernels, local(): pl.pallas_call(functools.partial(kernel, conv_weight.shape[1]), out_shape...  62.7 us
    unnamed x1, local copies, waits for them, and re-layouts  1.67 us

profile of v3, /device:TPU:1, one launch (start us, length us, event | category | flops | bytes accessed | tf_op | source)
XLA Modules:
  0.0 64.3 jit_solution(17308077949661815087)
XLA Ops:
  0.0 62.7 %shard_map.64 = bf16[128,1024]{1,0:T(8,128)(2,1)} custom-call(bf16[3,1024,128]{2,1,0:T(8,128)(2,1)} %streams_hbm.1, f32[3,7,1024]{2,1,0:T(8,128)} %taps_hbm.1, f32[16,128]{1,0:T(8,128)} %bitcast.3, f32[16,128]{1,0:T(8,128)} %bitcast.4, f32[1,1024]{1,0:T(1,128)} %bitcast.5, bf16[32,1024]{1,0:T(8,128)(2,1)} %w_hbm.1), custom_call_target="tpu_custom_call" | custom-call | flops 1073741824 | bytes 12582912 | tf_op jit(solution)/shard_map/pallas_call | solution.py:535
  62.7 1.7 %copy.8 = bf16[128,1024]{1,0:T(8,128)(2,1)} copy(bf16[128,1024]{1,0:T(8,128)(2,1)} %shard_map.64) | data formatting | bytes 524288

commit v4 on v3

--- a/solution.py
+++ b/solution.py
@@ -57,6 +57,7 @@
     query,
     gated,
     conv,
+    factors,
     decay,
     coef,
     rate_chunks,
@@ -69,6 +70,9 @@
     enter_out,
     enter_in,
     mixed,
+    outbox,
+    part_out,
+    part_back,
     total,
     load_sems,
     send_sems,
@@ -123,14 +127,17 @@
     def greet(peer):
         pl.semaphore_signal(barrier, inc=1, device_id=peer, device_id_type=pl.DeviceIdType.MESH)
 
+    sibling = at(core_=1 - core)[0]
     always = [at(y_=1 - y)]
-    always += [(ctx - place + flip(place, m), tp) for m in range(1, LINE)]
-    always += [at(z_=flip(z, m)) for m in range(1, NZ)]
+    always += [at(z_=flip(z, m)) for m in range(NZ - 1, 0, -1)]
+    always += [(ctx - place + flip(place, m), tp) for m in range(LINE - 1, 0, -1)]
     sometimes = [
         (ctx < ctx_n - 1, (ctx + 1, tp)),
         (ctx > 0, (ctx - 1, tp)),
         (tp < tp_n - 1, (ctx, tp + 1)),
         (tp > 0, (ctx, tp - 1)),
+        (tp < tp_n - 1, (sibling, tp + 1)),
+        (tp > 0, (sibling, tp - 1)),
     ]
     greetings = len(always)
     for peer in always:
@@ -160,7 +167,6 @@
     rights, lefts = at(x_=(x + 1) % NX), at(x_=(x + NX - 1) % NX)
     x_left, x_right = (x + NX - 1) % NX, (x + 1) % NX
     x_far = (x + 2) % NX
-    sibling = at(core_=1 - core)
     top, bottom = pl.ds(0, rows // 2), pl.ds(rows // 2, rows // 2)
     own, other = y, 1 - y
 
@@ -209,19 +215,12 @@
             pair += (message(w.at[own, down_src, x_, core], dst, dst, downs),)
         return pair
 
-    def share(y_, group):
-        slots = pl.ds(*groups[group])
-        mine = w.at[y_, slots, pl.ds(0, NX), core]
-        return (message(mine, mine, w.at[y_, slots, pl.ds(0, NX), 1 - core], sibling),)
-
     za_m = {s: za(s) for s in (1, 2, 3, 4)}
     xa_m = {g: xa(other, g) for g in range(5)}
     xaf_m = {g: xa_far(other, g) for g in range(5)}
     xb_m, xbf_m = xa(own, 0), xa_far(own, 0)
     chains = {"mine": (x, True), "left": (x_left, True), "right": (x_right, False), "far": (x_far, False)}
     zb_m = {(c, s): zb(s, *chains[c]) for c in chains for s in (1, 2, 3, 4)}
-    own_share = {g: share(own, g) for g in range(5)}
-    other_share = {g: share(other, g) for g in range(5)}
 
     def zb_next(chain, step):
         recv_all(zb_m[chain, step])
@@ -233,29 +232,46 @@
         == lax.broadcasted_iota(jnp.int32, (tokens, tokens), 1)
     ).astype(jnp.bfloat16)
     loads[0].wait()
-    loads[1].wait()
-    for s in range(3):
-        ext[s, pl.ds(RIM, tokens), :] = lax.dot_general(
-            eye, streams[s], (((1,), (1,)), ((), ())), preferred_element_type=jnp.float32
-        )
     pl.semaphore_wait(barrier, greetings)
-
-    pl.when(ctx < ctx_n - 1)(rim_m.start)
     start_all(xb_m)
     start_all(zb_m["mine", 1])
     start_all(across)
+    loads[1].wait()
+    for s in range(3):
+        pairs = streams[s].reshape(channels // (2 * rows), 2, rows, tokens)
+        for h in range(2):
+            ext[s, pl.ds(RIM, tokens), pl.ds(h * half, half)] = lax.dot_general(
+                eye, pairs[:, h].reshape(half, tokens), (((1,), (1,)), ((), ())), preferred_element_type=jnp.float32
+            )
+    pl.when(ctx < ctx_n - 1)(rim_m.start)
+
+    def channel_at(lane, half_width):
+        return (lane % half_width) // rows * (2 * rows) + lane // half_width * rows + lane % rows
 
     for load in loads[2:]:
         load.wait()
     group_count = rates.shape[1]
+    lane = lax.broadcasted_iota(jnp.int32, (group_count, channels), 1)
     spread = (
-        lax.broadcasted_iota(jnp.int32, (group_count, channels), 1) // (channels // group_count)
+        channel_at(lane, half) // (channels // group_count)
         == lax.broadcasted_iota(jnp.int32, (group_count, channels), 0)
     ).astype(jnp.float32)
     plain = (((1,), (0,)), ((), ()))
     rate = lax.dot_general(rates[...], spread, plain, precision=HIGHEST, preferred_element_type=jnp.float32)
     residue = lax.dot_general(residues[...], spread, plain, precision=HIGHEST, preferred_element_type=jnp.float32)
     decay[...] = jnp.exp(-rate)
+    two = 2 * LANES
+    order = (
+        channel_at(lax.broadcasted_iota(jnp.int32, (two, two), 1), LANES)
+        == lax.broadcasted_iota(jnp.int32, (two, two), 0)
+    ).astype(jnp.float32)
+    by_tap = jnp.concatenate([taps[s] for s in range(3)] + [skip[...]], axis=0)
+    for k in range(channels // two):
+        moved = lax.dot_general(
+            by_tap[:, k * two : (k + 1) * two], order, plain, precision=HIGHEST, preferred_element_type=jnp.float32
+        )
+        for h in range(2):
+            factors[:, pl.ds(h * half + k * LANES, LANES)] = moved[:, h * LANES : (h + 1) * LANES]
     coef[...] = residue * jnp.sqrt(2.0 * rate) * (1.0 / math.sqrt(poles))
     for k in range(LINE):
         rate_chunks[k] = rate[:, k * LANES : (k + 1) * LANES]
@@ -267,7 +283,7 @@
             def filtered(s):
                 total_ = None
                 for shift in range(tap_count):
-                    term = taps[s, pl.ds(shift, 1), lanes] * ext[s, pl.ds(RIM + first - shift, length), lanes]
+                    term = factors[pl.ds(s * tap_count + shift, 1), lanes] * ext[s, pl.ds(RIM + first - shift, length), lanes]
                     total_ = term if total_ is None else total_ + term
                 return total_
 
@@ -320,6 +336,9 @@
         round1.append(message(ends.at[to], line_in.at[place], line_in.at[to], (ctx - place + to, tp)))
     start_all(round1)
     line_in[place] = ends[place]
+    my_rate = rate_chunks[place]
+    block_fall = jnp.exp(my_rate * (-float(tokens)))
+    row_fall = jnp.exp(my_rate * (-float(tokens * LINE)))
 
     recv_all(xb_m)
     start_all(xbf_m)
@@ -328,9 +347,6 @@
     zb_next("mine", 1)
 
     recv_all(round1)
-    my_rate = rate_chunks[place]
-    block_fall = jnp.exp(my_rate * (-float(tokens)))
-    row_fall = jnp.exp(my_rate * (-float(tokens * LINE)))
     state = line_in[0]
     for p in range(1, LINE):
         state = state * block_fall + line_in[p]
@@ -348,7 +364,6 @@
     recv_all(across)
     start_all(za_m[1])
     start_all(xa_m[0])
-    zb_next("mine", 2)
 
     recv_all(round2)
     onward = message(part_total, part_in, part_in, at(y_=1 - y))
@@ -362,11 +377,12 @@
         onward.start()
         part_in[...] = jnp.zeros_like(part_in)
 
-    zb_next("left", 1)
-    zb_next("right", 1)
+    zb_next("mine", 2)
     recv_all(za_m[1])
     start_all(za_m[2])
     start_all(xa_m[1])
+    zb_next("left", 1)
+    zb_next("right", 1)
     recv_all(xa_m[0])
     start_all(xaf_m[0])
     zb_next("far", 1)
@@ -394,135 +410,151 @@
     start_all(za_m[3])
     start_all(xa_m[2])
     zb_next("mine", 3)
+    recv_all(xa_m[1])
+    start_all(xaf_m[1])
     zb_next("left", 2)
     zb_next("right", 2)
-    recv_all(xa_m[1])
-    start_all(xaf_m[1])
 
     recv_all(round3)
 
     right_m, left_m = {}, {}
-    for h in range(2):
+    up_tp, down_tp = (tp + 1) % tp_n, (tp + tp_n - 1) % tp_n
+    home = message(outbox, mixed.at[core, tp], mixed.at[1 - core, tp], (sibling, tp))
+    for r in range(2):
+        of = core if r == 0 else 1 - core
         for d in range(3):
             behind, ahead = (tp + tp_n - d) % tp_n, (tp + d) % tp_n
-            right_m[h, d] = message(
-                mixed.at[h, behind], mixed.at[h, behind], mixed.at[h, (tp + tp_n - 1 - d) % tp_n], (ctx, (tp + 1) % tp_n)
-            )
-            left_m[h, d] = message(
-                mixed.at[h, ahead], mixed.at[h, ahead], mixed.at[h, (tp + 1 + d) % tp_n], (ctx, (tp + tp_n - 1) % tp_n)
-            )
-
-    def line_send(h, d):
-        pl.when((tp < tp_n - 1) & (tp >= d))(right_m[h, d].start)
-        pl.when((tp > 0) & (tp + d < tp_n))(left_m[h, d].start)
-
-    def line_sent(h, d):
-        pl.when((tp < tp_n - 1) & (tp >= d))(right_m[h, d].sent)
-        pl.when((tp > 0) & (tp + d < tp_n))(left_m[h, d].sent)
-
-    def line_recv(h, d):
-        pl.when(tp >= d + 1)(right_m[h, d].recv)
-        pl.when(tp + d + 1 < tp_n)(left_m[h, d].recv)
-
-    for h in range(2):
-        lanes = halves[h]
+            from_left, from_right = mixed.at[of, (tp + tp_n - 1 - d) % tp_n], mixed.at[of, (tp + 1 + d) % tp_n]
+            if (r, d) == (1, 0):
+                right_m[r, d] = message(outbox, mixed.at[core, tp], from_left, (sibling, up_tp))
+                left_m[r, d] = message(outbox, mixed.at[core, tp], from_right, (sibling, down_tp))
+            else:
+                right_m[r, d] = message(mixed.at[of, behind], mixed.at[of, behind], from_left, (ctx, up_tp))
+                left_m[r, d] = message(mixed.at[of, ahead], mixed.at[of, ahead], from_right, (ctx, down_tp))
+
+    def line_send(r, d):
+        pl.when((tp < tp_n - 1) & (tp >= d))(right_m[r, d].start)
+        pl.when((tp > 0) & (tp + d < tp_n))(left_m[r, d].start)
+
+    def line_sent(r, d):
+        pl.when((tp < tp_n - 1) & (tp >= d))(right_m[r, d].sent)
+        pl.when((tp > 0) & (tp + d < tp_n))(left_m[r, d].sent)
+
+    def line_recv(r, d):
+        pl.when(tp >= d + 1)(right_m[r, d].recv)
+        pl.when(tp + d + 1 < tp_n)(left_m[r, d].recv)
+
+    for r in (1, 0):
+        which = core if r == 0 else 1 - core
+        lanes = pl.ds(pl.multiple_of(which * half, half), half)
         fall, gain = decay[:, lanes], coef[:, lanes]
-        first = h * (half // LANES)
+        first = which * (half // LANES)
         enter = jnp.concatenate([enter_in[first + k] for k in range(half // LANES)], axis=1)
 
         def step(t, state):
             for u in range(unroll):
                 at_t = pl.ds(t * unroll + u, 1)
                 state = state * fall + gated[at_t, lanes]
-                conv[at_t, lanes] = jnp.sum(state * gain, axis=0, keepdims=True)
+                conv[at_t, :] = jnp.sum(state * gain, axis=0, keepdims=True)
             return state
 
         lax.fori_loop(0, tokens // unroll, step, enter)
-        mixed[h, tp] = (
-            query[:, lanes] * (conv[:, lanes] + skip[:, lanes] * gated[:, lanes])
+        block = (
+            query[:, lanes] * (conv[...] + factors[pl.ds(3 * tap_count, 1), lanes] * gated[:, lanes])
         ).astype(jnp.bfloat16)
-        line_send(h, 0)
+        if r == 1:
+            outbox[...] = block
+            start_all((home,))
+        else:
+            mixed[core, tp] = block
+        line_send(r, 0)
 
     recv_all(za_m[3])
     start_all(za_m[4])
     start_all(xa_m[3])
     zb_next("far", 2)
-    zb_next("left", 3)
-    zb_next("right", 3)
     recv_all(xa_m[2])
     start_all(xaf_m[2])
-    start_all(own_share[0])
-    start_all(own_share[1])
-    start_all(own_share[2])
+    zb_next("left", 3)
+    line_recv(1, 0)
+    line_send(1, 1)
+    zb_next("right", 3)
+    recv_all(za_m[4])
+    start_all(xa_m[4])
+    recv_all(xa_m[3])
+    start_all(xaf_m[3])
+    zb_next("far", 3)
     line_recv(0, 0)
     line_send(0, 1)
-    recv_all(za_m[4])
-    start_all(xa_m[4])
-    zb_next("far", 3)
-    start_all(own_share[3])
-    line_recv(1, 0)
-    line_send(1, 1)
-    recv_all(xa_m[3])
-    start_all(xaf_m[3])
-    for g in range(3):
+    recv_all(xa_m[4])
+    start_all(xaf_m[4])
+    line_recv(1, 1)
+    line_send(1, 2)
+    recv_all((home,))
+
+    deep = NX * rows
+    total[...] = jnp.zeros_like(total)
+
+    def slot_of(z_):
+        behind = (z_ + NZ - z) % NZ
+        return jnp.where(behind <= 4, jnp.maximum(2 * behind - 1, 0), 2 * (NZ - behind))
+
+    last_pair = ((z + NZ // 2) % NZ) // 2
+
+    def project(distances, late):
+        def step(n, carry):
+            y_, pair = n // 4, n % 4
+            block = y_ * 2 + pair // 2
+            distance = jnp.maximum(block - tp, tp - block)
+            wanted = (distance >= distances[0]) & (distance <= distances[1])
+            if late is not None:
+                wanted = wanted & ((pair == last_pair) if late else (pair != last_pair))
+
+            @pl.when(wanted)
+            def _():
+                weights = jnp.concatenate(
+                    [
+                        w[y_, slot_of(2 * pair + k), pl.ds(0, NX), core].reshape(deep, w.shape[-1])
+                        for k in range(2)
+                    ],
+                    axis=0,
+                )
+                part = pl.ds(pl.multiple_of((pair % 2) * 2 * deep, 2 * deep), 2 * deep)
+                left = jnp.concatenate([mixed[c, block, :, part] for c in range(2)], axis=0)
+                total[...] += jnp.dot(left, weights, preferred_element_type=jnp.float32)
+
+            return carry
+
+        lax.fori_loop(0, 2 * NZ // 2, step, 0)
+
+    for g in range(4):
         recv_all(xaf_m[g])
-        start_all(other_share[g])
+    project((0, 0), False)
     line_recv(0, 1)
     line_send(0, 2)
-    recv_all(xa_m[4])
-    start_all(xaf_m[4])
+    project((1, 2), False)
+    recv_all(xaf_m[4])
     for c in chains:
         recv_all(zb_m[c, 4])
-    start_all(own_share[4])
-    line_recv(1, 1)
-    line_send(1, 2)
-    for g in range(3, 5):
-        recv_all(xaf_m[g])
-        start_all(other_share[g])
-    for g in range(5):
-        recv_all(own_share[g])
-        recv_all(other_share[g])
-
-    deep = LINE * rows
-
-    def project(h, block):
-        def step(k, carry):
-            place_ = block * 4 + h * 2 + k
-            y_, z_ = place_ // NZ, place_ % NZ
-            behind = (z_ + NZ - z) % NZ
-            slot = jnp.where(behind <= 4, jnp.maximum(2 * behind - 1, 0), 2 * (NZ - behind))
-            weights = w[y_, slot].reshape(deep, w.shape[-1])
-            part = pl.ds(pl.multiple_of(k * deep, deep), deep)
-            total[...] += jnp.dot(mixed[h, block, :, part], weights, preferred_element_type=jnp.float32)
-            return carry
-
-        lax.fori_loop(0, 2, step, 0)
-
-    total[...] = jnp.zeros_like(total)
-    for h in range(2):
-        project(h, tp)
-    for d in range(3):
-        for h in range(2):
-            if d == 2:
-                line_recv(h, d)
-
-            @pl.when(tp >= d + 1)
-            def _():
-                project(h, tp - 1 - d)
-
-            @pl.when(tp + d + 1 < tp_n)
-            def _():
-                project(h, tp + 1 + d)
-
-    out[...] = total[...].astype(jnp.bfloat16)
+    project((0, 2), True)
+    line_recv(1, 2)
+    line_recv(0, 2)
+    project((3, 3), None)
+
+    part_out[...] = total[pl.ds(pl.multiple_of((1 - core) * tokens, tokens), tokens), :].astype(jnp.bfloat16)
+    swap = message(part_out, part_back, part_back, (sibling, tp))
+    start_all((swap,))
+    recv_all((swap,))
+    mine = total[pl.ds(pl.multiple_of(core * tokens, tokens), tokens), :]
+    out[...] = (mine + part_back[...].astype(jnp.float32)).astype(jnp.bfloat16)
 
     for made in sent:
         made.sent()
     pl.when(ctx < ctx_n - 1)(rim_m.sent)
     pl.when(y == 0)(onward.sent)
-    for h in range(2):
+    for r in range(2):
         for d in range(3):
-            line_sent(h, d)
+            line_sent(r, d)
 
 
 def local(streams, conv_weight, rates, residues, skip, out_weight):
@@ -531,7 +563,7 @@
     rows, features = out_weight.shape
     anywhere = pl.BlockSpec(memory_space=pl.ANY)
     f32, bf16 = jnp.float32, jnp.bfloat16
-    messages = 1 + 8 + 20 + 4 + 28 + 10 + 1 + 7 + 7 + 1 + 7 + 12
+    messages = 1 + 8 + 20 + 4 + 28 + 1 + 7 + 7 + 1 + 7 + 13 + 1
     return pl.pallas_call(
         functools.partial(kernel, conv_weight.shape[1]),
         out_shape=jax.ShapeDtypeStruct((tokens, features), bf16),
@@ -547,7 +579,8 @@
             pltpu.VMEM((3, RIM + tokens, channels), f32),
             pltpu.VMEM((tokens, channels), f32),
             pltpu.VMEM((tokens, channels), f32),
-            pltpu.VMEM((tokens, channels), f32),
+            pltpu.VMEM((tokens, channels // 2), f32),
+            pltpu.VMEM((3 * conv_weight.shape[1] + 1, channels), f32),
             pltpu.VMEM((poles, channels), f32),
             pltpu.VMEM((poles, channels), f32),
             pltpu.VMEM((LINE, poles, LANES), f32),
@@ -560,7 +593,10 @@
             pltpu.VMEM((LINE, poles, LANES), f32),
             pltpu.VMEM((LINE, poles, LANES), f32),
             pltpu.VMEM((2, 4, tokens, channels // 2), bf16),
-            pltpu.VMEM((tokens, features), f32),
+            pltpu.VMEM((tokens, channels // 2), bf16),
+            pltpu.VMEM((tokens, features), bf16),
+            pltpu.VMEM((tokens, features), bf16),
+            pltpu.VMEM((2 * tokens, features), f32),
             pltpu.SemaphoreType.DMA((6,)),
             pltpu.SemaphoreType.DMA((messages,)),
             pltpu.SemaphoreType.DMA((messages,)),

time: 65.4 us -> 65.5 us (level)
  Pallas kernels: 62.7 us -> 63.4 us
    pallas_call x1, Pallas kernels: 62.7 us -> 63.4 us  [local(): pl.pallas_call(functools.partial(kernel, conv_weight.shape[1]), out_shape...]
where the time goes in v4:
time: 65.5 us; the launch traced here: 65 us
  Pallas kernels  63.4 us (97%)
  local copies, waits for them, and re-layouts  1.67 us (3%)
    pallas_call x1, Pallas kernels, local(): pl.pallas_call(functools.partial(kernel, conv_weight.shape[1]), out_shape...  63.4 us
    unnamed x1, local copies, waits for them, and re-layouts  1.67 us

profile of v4, /device:TPU:1, one launch (start us, length us, event | category | flops | bytes accessed | tf_op | source)
XLA Modules:
  0.0 65.0 jit_solution(10196934816500806314)
XLA Ops:
  0.0 63.4 %shard_map.64 = bf16[128,1024]{1,0:T(8,128)(2,1)} custom-call(bf16[3,1024,128]{2,1,0:T(8,128)(2,1)} %streams_hbm.1, f32[3,7,1024]{2,1,0:T(8,128)} %taps_hbm.1, f32[16,128]{1,0:T(8,128)} %bitcast.3, f32[16,128]{1,0:T(8,128)} %bitcast.4, f32[1,1024]{1,0:T(1,128)} %bitcast.5, bf16[32,1024]{1,0:T(8,128)(2,1)} %w_hbm.1), custom_call_target="tpu_custom_call" | custom-call | flops 1073741824 | bytes 12582912 | tf_op jit(solution)/shard_map/pallas_call | solution.py:567
  63.4 1.7 %copy.8 = bf16[128,1024]{1,0:T(8,128)(2,1)} copy(bf16[128,1024]{1,0:T(8,128)(2,1)} %shard_map.64) | data formatting | bytes 524288

commit v5 on v4

--- a/solution.py
+++ b/solution.py
@@ -74,6 +74,7 @@
     part_out,
     part_back,
     total,
+    heard,
     load_sems,
     send_sems,
     recv_sems,
@@ -128,32 +129,43 @@
         pl.semaphore_signal(barrier, inc=1, device_id=peer, device_id_type=pl.DeviceIdType.MESH)
 
     sibling = at(core_=1 - core)[0]
-    always = [at(y_=1 - y)]
-    always += [at(z_=flip(z, m)) for m in range(NZ - 1, 0, -1)]
+    ups, downs = at(z_=(z + 1) % NZ), at(z_=(z + NZ - 1) % NZ)
+    wraps_up, wraps_down = tp == tp_n - 1, tp == 0
+    crossed = (ctx + ctx_n // 2) % ctx_n
+    onwards = (jnp.where(wraps_up, crossed, ctx), jnp.where(wraps_up, 0, tp + 1))
+    backwards = (jnp.where(wraps_down, crossed, ctx), jnp.where(wraps_down, tp_n - 1, tp - 1))
+    always = [ups, downs, onwards, backwards]
     always += [(ctx - place + flip(place, m), tp) for m in range(LINE - 1, 0, -1)]
-    sometimes = [
-        (ctx < ctx_n - 1, (ctx + 1, tp)),
-        (ctx > 0, (ctx - 1, tp)),
-        (tp < tp_n - 1, (ctx, tp + 1)),
-        (tp > 0, (ctx, tp - 1)),
-        (tp < tp_n - 1, (sibling, tp + 1)),
-        (tp > 0, (sibling, tp - 1)),
-    ]
-    greetings = len(always)
     for peer in always:
         greet(peer)
-    for there, peer in sometimes:
-        pl.when(there)(functools.partial(greet, peer))
+    pl.when(ctx > 0)(functools.partial(greet, (ctx - 1, tp)))
+    pl.when(tp < tp_n - 1)(functools.partial(greet, (sibling, tp + 1)))
+    pl.when(tp > 0)(functools.partial(greet, (sibling, tp - 1)))
+    greetings = len(always)
+    for there in (ctx < ctx_n - 1, tp < tp_n - 1, tp > 0):
         greetings = greetings + there.astype(jnp.int32)
+
+    ways = [ups, downs, onwards]
+
+    def tell(way, step):
+        pl.semaphore_signal(
+            heard.at[way, step], inc=1, device_id=ways[way], device_id_type=pl.DeviceIdType.MESH
+        )
+
+    def pass_on(step):
+        for way in range(3):
+            pl.semaphore_wait(heard.at[way, step], 1)
+            if step < 2:
+                tell(way, step + 1)
 
     loads = [
         pltpu.make_async_copy(src, dst, load_sems.at[n])
         for n, (src, dst) in enumerate(
             [
+                (rates_hbm, rates),
+                (residues_hbm, residues),
                 (w_hbm, w.at[y, 0, x, core]),
                 (streams_hbm, streams),
-                (rates_hbm, rates),
-                (residues_hbm, residues),
                 (taps_hbm, taps),
                 (skip_hbm, skip),
             ]
@@ -163,7 +175,6 @@
         load.start()
 
     groups = [(0, 1), (1, 2), (3, 2), (5, 2), (7, 1)]
-    ups, downs = at(z_=(z + 1) % NZ), at(z_=(z + NZ - 1) % NZ)
     rights, lefts = at(x_=(x + 1) % NX), at(x_=(x + NX - 1) % NX)
     x_left, x_right = (x + NX - 1) % NX, (x + 1) % NX
     x_far = (x + 2) % NX
@@ -226,17 +237,40 @@
         recv_all(zb_m[chain, step])
         start_all(zb_m[chain, step + 1])
 
-    rim_m = message(ext.at[:, pl.ds(tokens, RIM), :], ext.at[:, pl.ds(0, RIM), :], ext.at[:, pl.ds(0, RIM), :], (ctx + 1, tp))
+    def channel_at(lane, half_width):
+        return (lane % half_width) // rows * (2 * rows) + lane // half_width * rows + lane % rows
+
+    plain = (((1,), (0,)), ((), ()))
+    group_count = rates.shape[1]
+    lane = lax.broadcasted_iota(jnp.int32, (group_count, channels), 1)
+    spread = (
+        channel_at(lane, half) // (channels // group_count)
+        == lax.broadcasted_iota(jnp.int32, (group_count, channels), 0)
+    ).astype(jnp.float32)
+    loads[0].wait()
+    loads[1].wait()
+    rate = lax.dot_general(rates[...], spread, plain, precision=HIGHEST, preferred_element_type=jnp.float32)
+    residue = lax.dot_general(residues[...], spread, plain, precision=HIGHEST, preferred_element_type=jnp.float32)
+    decay[...] = jnp.exp(-rate)
+    coef[...] = residue * jnp.sqrt(2.0 * rate) * (1.0 / math.sqrt(poles))
+    for k in range(LINE):
+        rate_chunks[k] = rate[:, k * LANES : (k + 1) * LANES]
+
+    loads[2].wait()
+    pl.semaphore_wait(barrier, greetings)
+    for way in range(3):
+        tell(way, 0)
+    start_all(xb_m)
+    start_all(zb_m["mine", 1])
+
+    rim_m = message(
+        ext.at[:, pl.ds(tokens, RIM), :], ext.at[:, pl.ds(0, RIM), :], ext.at[:, pl.ds(0, RIM), :], (ctx + 1, tp)
+    )
     eye = (
         lax.broadcasted_iota(jnp.int32, (tokens, tokens), 0)
         == lax.broadcasted_iota(jnp.int32, (tokens, tokens), 1)
     ).astype(jnp.bfloat16)
-    loads[0].wait()
-    pl.semaphore_wait(barrier, greetings)
-    start_all(xb_m)
-    start_all(zb_m["mine", 1])
-    start_all(across)
-    loads[1].wait()
+    loads[3].wait()
     for s in range(3):
         pairs = streams[s].reshape(channels // (2 * rows), 2, rows, tokens)
         for h in range(2):
@@ -244,27 +278,15 @@
                 eye, pairs[:, h].reshape(half, tokens), (((1,), (1,)), ((), ())), preferred_element_type=jnp.float32
             )
     pl.when(ctx < ctx_n - 1)(rim_m.start)
-
-    def channel_at(lane, half_width):
-        return (lane % half_width) // rows * (2 * rows) + lane // half_width * rows + lane % rows
-
-    for load in loads[2:]:
-        load.wait()
-    group_count = rates.shape[1]
-    lane = lax.broadcasted_iota(jnp.int32, (group_count, channels), 1)
-    spread = (
-        channel_at(lane, half) // (channels // group_count)
-        == lax.broadcasted_iota(jnp.int32, (group_count, channels), 0)
-    ).astype(jnp.float32)
-    plain = (((1,), (0,)), ((), ()))
-    rate = lax.dot_general(rates[...], spread, plain, precision=HIGHEST, preferred_element_type=jnp.float32)
-    residue = lax.dot_general(residues[...], spread, plain, precision=HIGHEST, preferred_element_type=jnp.float32)
-    decay[...] = jnp.exp(-rate)
+    pass_on(0)
+
     two = 2 * LANES
     order = (
         channel_at(lax.broadcasted_iota(jnp.int32, (two, two), 1), LANES)
         == lax.broadcasted_iota(jnp.int32, (two, two), 0)
     ).astype(jnp.float32)
+    loads[4].wait()
+    loads[5].wait()
     by_tap = jnp.concatenate([taps[s] for s in range(3)] + [skip[...]], axis=0)
     for k in range(channels // two):
         moved = lax.dot_general(
@@ -272,9 +294,6 @@
         )
         for h in range(2):
             factors[:, pl.ds(h * half + k * LANES, LANES)] = moved[:, h * LANES : (h + 1) * LANES]
-    coef[...] = residue * jnp.sqrt(2.0 * rate) * (1.0 / math.sqrt(poles))
-    for k in range(LINE):
-        rate_chunks[k] = rate[:, k * LANES : (k + 1) * LANES]
 
     def short_rows(first, length):
         def short(k, carry):
@@ -307,12 +326,16 @@
         return lax.fori_loop(0, length // unroll, step, state)
 
     short_rows(RIM, tokens - RIM)
+    pass_on(1)
     halves = [pl.ds(h * half, half) for h in range(2)]
     zeros = jnp.zeros((poles, half), jnp.float32)
     for h in range(2):
         state = run_states(RIM, tokens - RIM, halves[h], zeros)
         for k in range(half // LANES):
             ends[h * (half // LANES) + k] = state[:, k * LANES : (k + 1) * LANES]
+
+    pass_on(2)
+    start_all(across)
 
     @pl.when(ctx > 0)
     def _():
@@ -499,9 +522,12 @@
         behind = (z_ + NZ - z) % NZ
         return jnp.where(behind <= 4, jnp.maximum(2 * behind - 1, 0), 2 * (NZ - behind))
 
+    def tokens_of(c):
+        return pl.ds(pl.multiple_of(c * tokens, tokens), tokens)
+
     last_pair = ((z + NZ // 2) % NZ) // 2
 
-    def project(distances, late):
+    def project(distances, late, only=None):
         def step(n, carry):
             y_, pair = n // 4, n % 4
             block = y_ * 2 + pair // 2
@@ -520,8 +546,13 @@
                     axis=0,
                 )
                 part = pl.ds(pl.multiple_of((pair % 2) * 2 * deep, 2 * deep), 2 * deep)
-                left = jnp.concatenate([mixed[c, block, :, part] for c in range(2)], axis=0)
-                total[...] += jnp.dot(left, weights, preferred_element_type=jnp.float32)
+                if only is None:
+                    left = jnp.concatenate([mixed[c, block, :, part] for c in range(2)], axis=0)
+                    total[...] += jnp.dot(left, weights, preferred_element_type=jnp.float32)
+                else:
+                    total[tokens_of(only), :] += jnp.dot(
+                        mixed[only, block, :, part], weights, preferred_element_type=jnp.float32
+                    )
 
             return carry
 
@@ -538,15 +569,14 @@
         recv_all(zb_m[c, 4])
     project((0, 2), True)
     line_recv(1, 2)
-    line_recv(0, 2)
-    project((3, 3), None)
-
-    part_out[...] = total[pl.ds(pl.multiple_of((1 - core) * tokens, tokens), tokens), :].astype(jnp.bfloat16)
+    project((3, 3), None, 1 - core)
+    part_out[...] = total[tokens_of(1 - core), :].astype(jnp.bfloat16)
     swap = message(part_out, part_back, part_back, (sibling, tp))
     start_all((swap,))
+    line_recv(0, 2)
+    project((3, 3), None, core)
     recv_all((swap,))
-    mine = total[pl.ds(pl.multiple_of(core * tokens, tokens), tokens), :]
-    out[...] = (mine + part_back[...].astype(jnp.float32)).astype(jnp.bfloat16)
+    out[...] = (total[tokens_of(core), :] + part_back[...].astype(jnp.float32)).astype(jnp.bfloat16)
 
     for made in sent:
         made.sent()
@@ -597,6 +627,7 @@
             pltpu.VMEM((tokens, features), bf16),
             pltpu.VMEM((tokens, features), bf16),
             pltpu.VMEM((2 * tokens, features), f32),
+            pltpu.SemaphoreType.REGULAR((3, 3)),
             pltpu.SemaphoreType.DMA((6,)),
             pltpu.SemaphoreType.DMA((messages,)),
             pltpu.SemaphoreType.DMA((messages,)),

time: 65.5 us -> 62.5 us (0.954)
  Pallas kernels: 63.4 us -> 60.7 us
    pallas_call x1, Pallas kernels: 63.4 us -> 60.7 us  [local(): pl.pallas_call(functools.partial(kernel, conv_weight.shape[1]), out_shape...]
where the time goes in v5:
time: 62.5 us; the launch traced here: 62.4 us
  Pallas kernels  60.7 us (97%)
  local copies, waits for them, and re-layouts  1.67 us (3%)
    pallas_call x1, Pallas kernels, local(): pl.pallas_call(functools.partial(kernel, conv_weight.shape[1]), out_shape...  60.7 us
    unnamed x1, local copies, waits for them, and re-layouts  1.67 us

profile of v5, /device:TPU:1, one launch (start us, length us, event | category | flops | bytes accessed | tf_op | source)
XLA Modules:
  0.0 62.4 jit_solution(10592359705480662712)
XLA Ops:
  0.0 60.7 %shard_map.64 = bf16[128,1024]{1,0:T(8,128)(2,1)} custom-call(bf16[3,1024,128]{2,1,0:T(8,128)(2,1)} %streams_hbm.1, f32[3,7,1024]{2,1,0:T(8,128)} %taps_hbm.1, f32[16,128]{1,0:T(8,128)} %bitcast.3, f32[16,128]{1,0:T(8,128)} %bitcast.4, f32[1,1024]{1,0:T(1,128)} %bitcast.5, bf16[32,1024]{1,0:T(8,128)(2,1)} %w_hbm.1), custom_call_target="tpu_custom_call" | custom-call | flops 1073741824 | bytes 12582912 | tf_op jit(solution)/shard_map/pallas_call | solution.py:597
  60.7 1.7 %copy.8 = bf16[128,1024]{1,0:T(8,128)(2,1)} copy(bf16[128,1024]{1,0:T(8,128)(2,1)} %shard_map.64) | data formatting | bytes 524288

commit v6 on v5

--- a/solution.py
+++ b/solution.py
@@ -67,6 +67,7 @@
     row_in,
     part_total,
     part_in,
+    since,
     enter_out,
     enter_in,
     mixed,
@@ -146,6 +147,7 @@
         greetings = greetings + there.astype(jnp.int32)
 
     ways = [ups, downs, onwards]
+    last_step = [2, 2, 3]
 
     def tell(way, step):
         pl.semaphore_signal(
@@ -154,8 +156,9 @@
 
     def pass_on(step):
         for way in range(3):
-            pl.semaphore_wait(heard.at[way, step], 1)
-            if step < 2:
+            if step <= last_step[way]:
+                pl.semaphore_wait(heard.at[way, step], 1)
+            if step < last_step[way]:
                 tell(way, step + 1)
 
     loads = [
@@ -365,9 +368,10 @@
 
     recv_all(xb_m)
     start_all(xbf_m)
+    start_all(zb_m["right", 1])
     start_all(zb_m["left", 1])
-    start_all(zb_m["right", 1])
     zb_next("mine", 1)
+    pass_on(3)
 
     recv_all(round1)
     state = line_in[0]
@@ -389,7 +393,12 @@
     start_all(xa_m[0])
 
     recv_all(round2)
-    onward = message(part_total, part_in, part_in, at(y_=1 - y))
+    onward = []
+    for m in range(LINE):
+        far = flip(place, m)
+        onward.append(
+            message(part_total, part_in.at[place], part_in.at[far], ((ctx - place + far + ctx_n // 2) % ctx_n, tp))
+        )
 
     @pl.when(y == 0)
     def _():
@@ -397,24 +406,10 @@
         for r in range(1, NZ):
             state = state * row_fall + row_in[r]
         part_total[...] = state
-        onward.start()
-        part_in[...] = jnp.zeros_like(part_in)
-
-    zb_next("mine", 2)
-    recv_all(za_m[1])
-    start_all(za_m[2])
-    start_all(xa_m[1])
-    zb_next("left", 1)
-    zb_next("right", 1)
-    recv_all(xa_m[0])
-    start_all(xaf_m[0])
-    zb_next("far", 1)
-
-    @pl.when(y == 1)
-    def _():
-        onward.recv()
-
-    state = part_in[...]
+        for made in onward:
+            made.start()
+
+    state = jnp.zeros((poles, LANES), jnp.float32)
     for r in range(NZ - 1):
         state = jnp.where(r < z, state * row_fall + row_in[r], state)
     for p in range(LINE):
@@ -429,16 +424,27 @@
     start_all(round3)
     enter_in[place] = enter_out[place]
 
-    recv_all(za_m[2])
-    start_all(za_m[3])
-    start_all(xa_m[2])
-    zb_next("mine", 3)
-    recv_all(xa_m[1])
-    start_all(xaf_m[1])
-    zb_next("left", 2)
-    zb_next("right", 2)
+    zb_next("right", 1)
+    zb_next("left", 1)
+    recv_all(za_m[1])
+    start_all(za_m[2])
+    start_all(xa_m[1])
+    recv_all(xa_m[0])
+    start_all(xaf_m[0])
+    zb_next("far", 1)
+    zb_next("mine", 2)
 
     recv_all(round3)
+
+    @pl.when(y == 1)
+    def _():
+        blocks = (ctx % (ctx_n // 2) * tokens).astype(jnp.float32)
+        for n in range(LINE):
+            since[n] = jnp.exp(rate_chunks[n] * -blocks)
+        recv_all(onward)
+        for n in range(LINE):
+            enter_in[n] += since[n] * part_in[n]
+
 
     right_m, left_m = {}, {}
     up_tp, down_tp = (tp + 1) % tp_n, (tp + tp_n - 1) % tp_n
@@ -491,6 +497,14 @@
         else:
             mixed[core, tp] = block
         line_send(r, 0)
+        if r == 1:
+            recv_all(za_m[2])
+            start_all(za_m[3])
+            start_all(xa_m[2])
+            zb_next("right", 2)
+            zb_next("left", 2)
+            recv_all(xa_m[1])
+            start_all(xaf_m[1])
 
     recv_all(za_m[3])
     start_all(za_m[4])
@@ -498,17 +512,18 @@
     zb_next("far", 2)
     recv_all(xa_m[2])
     start_all(xaf_m[2])
-    zb_next("left", 3)
+    zb_next("mine", 3)
     line_recv(1, 0)
     line_send(1, 1)
     zb_next("right", 3)
     recv_all(za_m[4])
     start_all(xa_m[4])
-    recv_all(xa_m[3])
-    start_all(xaf_m[3])
+    zb_next("left", 3)
     zb_next("far", 3)
     line_recv(0, 0)
     line_send(0, 1)
+    recv_all(xa_m[3])
+    start_all(xaf_m[3])
     recv_all(xa_m[4])
     start_all(xaf_m[4])
     line_recv(1, 1)
@@ -581,7 +596,12 @@
     for made in sent:
         made.sent()
     pl.when(ctx < ctx_n - 1)(rim_m.sent)
-    pl.when(y == 0)(onward.sent)
+
+    @pl.when(y == 0)
+    def _():
+        for made in onward:
+            made.sent()
+
     for r in range(2):
         for d in range(3):
             line_sent(r, d)
@@ -593,7 +613,7 @@
     rows, features = out_weight.shape
     anywhere = pl.BlockSpec(memory_space=pl.ANY)
     f32, bf16 = jnp.float32, jnp.bfloat16
-    messages = 1 + 8 + 20 + 4 + 28 + 1 + 7 + 7 + 1 + 7 + 13 + 1
+    messages = 1 + 8 + 20 + 4 + 28 + 1 + 7 + 7 + 8 + 7 + 13 + 1
     return pl.pallas_call(
         functools.partial(kernel, conv_weight.shape[1]),
         out_shape=jax.ShapeDtypeStruct((tokens, features), bf16),
@@ -619,7 +639,8 @@
             pltpu.VMEM((poles, LANES), f32),
             pltpu.VMEM((NZ, poles, LANES), f32),
             pltpu.VMEM((poles, LANES), f32),
-            pltpu.VMEM((poles, LANES), f32),
+            pltpu.VMEM((LINE, poles, LANES), f32),
+            pltpu.VMEM((LINE, poles, LANES), f32),
             pltpu.VMEM((LINE, poles, LANES), f32),
             pltpu.VMEM((LINE, poles, LANES), f32),
             pltpu.VMEM((2, 4, tokens, channels // 2), bf16),
@@ -627,7 +648,7 @@
             pltpu.VMEM((tokens, features), bf16),
             pltpu.VMEM((tokens, features), bf16),
             pltpu.VMEM((2 * tokens, features), f32),
-            pltpu.SemaphoreType.REGULAR((3, 3)),
+            pltpu.SemaphoreType.REGULAR((3, 4)),
             pltpu.SemaphoreType.DMA((6,)),
             pltpu.SemaphoreType.DMA((messages,)),
             pltpu.SemaphoreType.DMA((messages,)),

time: 62.5 us -> 58.6 us (0.938)
  Pallas kernels: 60.7 us -> 56.8 us
    pallas_call x1, Pallas kernels: 60.7 us -> 56.8 us  [local(): pl.pallas_call(functools.partial(kernel, conv_weight.shape[1]), out_shape...]
where the time goes in v6:
time: 58.6 us; the launch traced here: 58.5 us
  Pallas kernels  56.8 us (97%)
  local copies, waits for them, and re-layouts  1.67 us (3%)
    pallas_call x1, Pallas kernels, local(): pl.pallas_call(functools.partial(kernel, conv_weight.shape[1]), out_shape...  56.8 us
    unnamed x1, local copies, waits for them, and re-layouts  1.67 us

profile of v6, /device:TPU:1, one launch (start us, length us, event | category | flops | bytes accessed | tf_op | source)
XLA Modules:
  0.0 58.5 jit_solution(1956391400313832147)
XLA Ops:
  0.0 56.8 %shard_map.64 = bf16[128,1024]{1,0:T(8,128)(2,1)} custom-call(bf16[3,1024,128]{2,1,0:T(8,128)(2,1)} %streams_hbm.1, f32[3,7,1024]{2,1,0:T(8,128)} %taps_hbm.1, f32[16,128]{1,0:T(8,128)} %bitcast.3, f32[16,128]{1,0:T(8,128)} %bitcast.4, f32[1,1024]{1,0:T(1,128)} %bitcast.5, bf16[32,1024]{1,0:T(8,128)(2,1)} %w_hbm.1), custom_call_target="tpu_custom_call" | custom-call | flops 1073741824 | bytes 12582912 | tf_op jit(solution)/shard_map/pallas_call | solution.py:617
  56.8 1.7 %copy.8 = bf16[128,1024]{1,0:T(8,128)(2,1)} copy(bf16[128,1024]{1,0:T(8,128)(2,1)} %shard_map.64) | data formatting | bytes 524288

commit v7 on v6

--- a/solution.py
+++ b/solution.py
@@ -281,7 +281,6 @@
                 eye, pairs[:, h].reshape(half, tokens), (((1,), (1,)), ((), ())), preferred_element_type=jnp.float32
             )
     pl.when(ctx < ctx_n - 1)(rim_m.start)
-    pass_on(0)
 
     two = 2 * LANES
     order = (
@@ -328,6 +327,7 @@
 
         return lax.fori_loop(0, length // unroll, step, state)
 
+    pass_on(0)
     short_rows(RIM, tokens - RIM)
     pass_on(1)
     halves = [pl.ds(h * half, half) for h in range(2)]

time: 58.6 us -> 58.3 us (level)
  no operation moved by 1% of the time
where the time goes in v7:
time: 58.3 us; the launch traced here: 58.1 us
  Pallas kernels  56.4 us (97%)
  local copies, waits for them, and re-layouts  1.67 us (3%)
    pallas_call x1, Pallas kernels, local(): pl.pallas_call(functools.partial(kernel, conv_weight.shape[1]), out_shape...  56.4 us
    unnamed x1, local copies, waits for them, and re-layouts  1.67 us

profile of v7, /device:TPU:1, one launch (start us, length us, event | category | flops | bytes accessed | tf_op | source)
XLA Modules:
  0.0 58.1 jit_solution(13100365426208290193)
XLA Ops:
  0.0 56.4 %shard_map.64 = bf16[128,1024]{1,0:T(8,128)(2,1)} custom-call(bf16[3,1024,128]{2,1,0:T(8,128)(2,1)} %streams_hbm.1, f32[3,7,1024]{2,1,0:T(8,128)} %taps_hbm.1, f32[16,128]{1,0:T(8,128)} %bitcast.3, f32[16,128]{1,0:T(8,128)} %bitcast.4, f32[1,1024]{1,0:T(1,128)} %bitcast.5, bf16[32,1024]{1,0:T(8,128)(2,1)} %w_hbm.1), custom_call_target="tpu_custom_call" | custom-call | flops 1073741824 | bytes 12582912 | tf_op jit(solution)/shard_map/pallas_call | solution.py:617
  56.4 1.7 %copy.8 = bf16[128,1024]{1,0:T(8,128)(2,1)} copy(bf16[128,1024]{1,0:T(8,128)(2,1)} %shard_map.64) | data formatting | bytes 524288
